TPU v7x, 128 devices: a whole 4x4x4 slice. The times are simulated.
128 devices in a mesh: dp: 16 (over y_lo, z, core), tensor: 8 (over x, y_hi).
Axes of the slice: x: 4, y: 4 (y_hi: 2, y_lo: 2; y = y_hi * 2 + y_lo), z: 4, core: 2. Of those that a mesh axis runs over, the one named last changes fastest.
Arguments:
- normed: bfloat16 [8192, 8192], P('dp', 'tensor'), may hold values from -6 to 6
- query_back: bfloat16 [8192, 4096], P('dp', 'tensor'), may hold values from -1.5 to 1.5
- key_back: bfloat16 [8192, 1024], P('dp', 'tensor'), may hold values from -3 to 3
- value_back: bfloat16 [8192, 1024], P('dp', 'tensor'), may hold values from -3 to 3
- query_proj: bfloat16 [8192, 4096], P(None, 'tensor'), may hold values from -0.0625 to 0.0625
- key_proj: bfloat16 [8192, 1024], P(None, 'tensor'), may hold values from -0.0625 to 0.0625
- value_proj: bfloat16 [8192, 1024], P(None, 'tensor'), may hold values from -0.0625 to 0.0625
- source: int32 [4096], replicated, may hold values from 0 to 8191, as said below
Outputs:
- query_grad: float32 [8192, 4096], P('dp', 'tensor')
- key_grad: float32 [8192, 1024], P('dp', 'tensor')
- value_grad: float32 [8192, 1024], P('dp', 'tensor')
- input_grad: float32 [4096, 8192], P('dp', 'tensor')
Inputs may be any that keep to these rules, and one draw needn't show every extreme that they name: Each arrival device of the dp axis holds its live rows in its first slots; every live slot appears exactly once in source, no other slot appears. Every balanced device takes the same number of rows from a given arrival device, in one run of consecutive slots, runs ordered by arrival device; this number is at most 32 and equals 32 for at least one arrival device. Each balanced device holds 256 rows.
All inputs are finite; a program needn't handle non-finite values.
Results may differ from a plain program's by a relative error of at most 0.0003.
Values may be sent and summed in bfloat16 or wider, within the bound.
No kernel may reach another device: no remote copies, remote signals or barrier semaphores. Data moves between devices by JAX's collectives and lax.ppermute only.
A program may use at most 192 MiB of HBM per device.

v0:
```python
import functools
import itertools

import jax
import jax.numpy as jnp
from jax import lax
from jax.experimental import pallas as pl
from jax.experimental.pallas import tpu as pltpu
from jax.sharding import Mesh, PartitionSpec as P

DP_SIZES = (("y_lo", 2), ("z", 4), ("core", 2))
TENSOR_SIZES = (("x", 4), ("y_hi", 2))
DP = tuple(name for name, _ in DP_SIZES)
TENSOR = tuple(name for name, _ in TENSOR_SIZES)
SCALE_ROWS = 16
FRACTION_BITS = 15


def balanced_slots(source, dp_count, per_pair):
    owners = source[: source.shape[0] // dp_count] // (dp_count * per_pair)
    owner_start = jnp.sum((owners[None, :] < owners[:, None]).astype(jnp.int32), axis=1)
    return owners * per_pair + jnp.arange(owners.shape[0], dtype=jnp.int32) - owner_start


def pack_kernel(per_pair, me_ref, slots_ref, *refs):
    *value_refs, out_ref = refs
    slots = slots_ref[...]
    me = me_ref[0]
    count, width = slots.shape
    capacity = value_refs[0].shape[0]
    first_row = me * capacity
    lead = slots[:1, :]
    before = jnp.sum((lead < first_row).astype(jnp.float32)).astype(jnp.int32)
    mine = jnp.sum(((lead >= first_row) & (lead < first_row + capacity)).astype(jnp.float32)).astype(jnp.int32)
    moved = pltpu.roll(slots, (width - before) % width, axis=1)
    lane = lax.broadcasted_iota(jnp.int32, slots.shape, 1)
    picked = jnp.where(lane < mine, moved - first_row + 1, 0)
    picked = jnp.concatenate([picked, jnp.zeros((count, capacity - width), jnp.int32)], axis=1)
    reach = per_pair
    while reach < capacity:
        picked = picked + pltpu.roll(picked, reach, axis=1)
        reach *= 2
    row = lax.broadcasted_iota(jnp.int32, picked.shape, 0)
    lane = lax.broadcasted_iota(jnp.int32, picked.shape, 1)
    own = (lane >= row * per_pair) & (lane < (row + 1) * per_pair)
    rows = jnp.sum(jnp.where(own, picked, 0).astype(jnp.float32), axis=0, keepdims=True).astype(jnp.int32) - 1
    chosen = lax.broadcasted_iota(jnp.int32, (capacity, capacity), 0) == rows
    chosen = jnp.where(chosen, 1.0, 0.0).astype(out_ref.dtype)
    first = 0
    for ref in value_refs:
        taken = lax.dot_general(chosen, ref[...], (((0,), (0,)), ((), ())), preferred_element_type=jnp.float32)
        out_ref[:, first : first + ref.shape[1]] = taken.astype(out_ref.dtype)
        first += ref.shape[1]


def pack_rows(source, my_index, dp_count, per_pair, values):
    capacity = values[0].shape[0]
    width = sum(v.shape[1] for v in values)
    slots = source.reshape(dp_count, -1)
    whole = lambda shape: pl.BlockSpec(shape, lambda g, me_ref: (0, 0))
    return pl.pallas_call(
        functools.partial(pack_kernel, per_pair),
        grid_spec=pltpu.PrefetchScalarGridSpec(
            num_scalar_prefetch=1,
            grid=(1,),
            in_specs=[whole(v.shape) for v in (slots, *values)],
            out_specs=whole((capacity, width)),
        ),
        out_shape=jax.ShapeDtypeStruct((capacity, width), values[0].dtype),
        compiler_params=pltpu.CompilerParams(vmem_limit_bytes=60 * 2**20),
    )(my_index.reshape(1), slots, *values)


def take_rows(values, rows):
    chosen = (rows[:, None] == jnp.arange(values.shape[0], dtype=jnp.int32)[None, :]).astype(values.dtype)
    return jnp.dot(chosen, values, preferred_element_type=jnp.float32).astype(values.dtype)


def take_rows_across(values, rows):
    chosen = (rows[:, None] == jnp.arange(values.shape[0], dtype=jnp.int32)[None, :]).astype(values.dtype)
    contract = (((0,), (1,)), ((), ()))
    return lax.dot_general(values, chosen, contract, preferred_element_type=jnp.float32).astype(values.dtype)


def column_of(row_values, tokens):
    return jnp.transpose(jnp.broadcast_to(row_values, (128, tokens)))[:, :1]


def partial_kernel(sizes, arrivals, coded_out, order_ref, rows_ref, query_ref, key_ref, value_ref, *refs):
    contract = (((1,), (1,)), ((), ()))
    query_width = query_ref.shape[1]
    tokens = rows_ref.shape[0]
    step_index = pl.program_id(0)
    part = lax.dot_general(
        rows_ref[:, :query_width], query_ref[...], contract, preferred_element_type=jnp.float32
    )
    others = jnp.concatenate([key_ref[...], value_ref[...]], axis=1)
    part = part + lax.dot_general(
        rows_ref[:, query_width:], others, contract, preferred_element_type=jnp.float32
    )
    for ref in refs[:arrivals]:
        exponent = ref[0, tokens:, :tokens].astype(jnp.int32).astype(jnp.float32)[:1]
        step = jnp.exp2(column_of(exponent, tokens) - FRACTION_BITS)
        part = part + ref[0, :tokens, :].astype(jnp.int32).astype(jnp.float32) * step
    if not coded_out:
        refs[-1][0] = part
        return
    most = jnp.max(jnp.abs(part), axis=1, keepdims=True)
    exponent = jnp.floor(jnp.log2(jnp.maximum(most, 2.0**-100))) + 1.0
    coded = jnp.round(part * jnp.exp2(FRACTION_BITS - exponent))
    coded = jnp.clip(coded, -32767.0, 32767.0).astype(jnp.int32).astype(jnp.int16)
    across = jnp.transpose(jnp.broadcast_to(exponent, (tokens, 128)))[:SCALE_ROWS, :]
    width = coded.shape[1]
    across = jnp.concatenate([across, jnp.zeros((SCALE_ROWS, width - tokens), jnp.float32)], axis=1)
    across = across.astype(jnp.int32).astype(jnp.int16)
    first = 0
    for size, out_ref in zip(sizes, refs[arrivals:]):

        @pl.when((step_index >= first) & (step_index < first + size))
        def _(out_ref=out_ref):
            out_ref[0, :tokens, :] = coded
            out_ref[0, tokens:, :] = across

        first += size


def partials(order, sizes, rows, projections, features, arrived=(), places=None, coded_out=True):
    tokens, width = rows.shape
    steps = sum(sizes)
    coded_block = (1, tokens + SCALE_ROWS, features)
    out_block = coded_block if coded_out else (1, tokens, features)
    kind = jnp.int16 if coded_out else jnp.float32
    plan = [order]
    column = lambda values: plan.append(values.astype(jnp.int32)) or len(plan) - 1
    chosen = lambda g, plan_ref: (plan_ref[g], 0)
    in_turn = lambda first, size: lambda g, plan_ref: (jnp.clip(g - first, 0, size - 1), 0, 0)
    listed = lambda at: lambda g, plan_ref: (plan_ref[at * steps + g], 0, 0)
    arrived_specs = [pl.BlockSpec(coded_block, listed(column(blocks))) for _, blocks in arrived]
    if places is None:
        firsts = [sum(sizes[:i]) for i in range(len(sizes))]
        out_specs = [pl.BlockSpec(out_block, in_turn(f, n)) for f, n in zip(firsts, sizes)]
        out_counts = sizes
    else:
        out_specs = [pl.BlockSpec(out_block, listed(column(places)))]
        out_counts = (places.shape[0] + 1,)
    return pl.pallas_call(
        functools.partial(partial_kernel, sizes, len(arrived), coded_out),
        grid_spec=pltpu.PrefetchScalarGridSpec(
            num_scalar_prefetch=1,
            grid=(steps,),
            in_specs=[pl.BlockSpec((tokens, width), lambda g, plan_ref: (0, 0))]
            + [pl.BlockSpec((features, p.shape[1]), chosen) for p in projections]
            + arrived_specs,
            out_specs=out_specs,
        ),
        out_shape=[jax.ShapeDtypeStruct((n,) + out_block[1:], kind) for n in out_counts],
        compiler_params=pltpu.CompilerParams(vmem_limit_bytes=56 * 2**20),
    )(jnp.concatenate(plan), rows, *projections, *(values for values, _ in arrived))


def sum_kernel(plan_ref, here_ref, *refs):
    out_ref = refs[-1]
    tokens = here_ref.shape[0]
    total = here_ref[...]
    for exponent_ref, coded_ref in zip(refs[:-1:2], refs[1:-1:2]):
        exponent = exponent_ref[0].astype(jnp.int32).astype(jnp.float32)[:1]
        step = jnp.exp2(column_of(exponent, tokens) - FRACTION_BITS)
        total = total + coded_ref[0].astype(jnp.int32).astype(jnp.float32) * step
    out_ref[...] = total


def decoded_sum(here, arrived, places):
    tokens, features = here.shape
    step = features // 2
    columns = pl.BlockSpec((tokens, step), lambda j, plan_ref: (0, j))
    in_specs, operands = [columns], [here]
    for i in range(places.shape[0]):
        in_specs.append(
            pl.BlockSpec((1, SCALE_ROWS, tokens), lambda j, plan_ref, i=i: (plan_ref[i], tokens // SCALE_ROWS, 0))
        )
        in_specs.append(pl.BlockSpec((1, tokens, step), lambda j, plan_ref, i=i: (plan_ref[i], 0, j)))
        operands += [arrived, arrived]
    return pl.pallas_call(
        sum_kernel,
        grid_spec=pltpu.PrefetchScalarGridSpec(
            num_scalar_prefetch=1, grid=(features // step,), in_specs=in_specs, out_specs=columns
        ),
        out_shape=jax.ShapeDtypeStruct((tokens, features), jnp.float32),
        compiler_params=pltpu.CompilerParams(vmem_limit_bytes=60 * 2**20),
    )(places, *operands)


def weight_kernel(plan_ref, pair_ref, right_ref, far_0_ref, far_1_ref, left_ref, back_ref, *out_refs):
    half, tokens = out_refs[0].shape[0], pair_ref.shape[2]
    refs = [(pair_ref, 0), (pair_ref, 1), (right_ref, 0), (right_ref, 1)]
    refs += [(far_0_ref, 0), (far_1_ref, 0), (left_ref, 0), (left_ref, 1)]
    for which, out_ref in zip((1 - plan_ref[0], plan_ref[0]), out_refs):
        mine = pl.ds(pl.multiple_of(which * half, half), half)
        total = 0.0
        for i, (ref, e) in enumerate(refs):
            rows = pl.ds(pl.multiple_of(plan_ref[1 + i] * tokens, tokens), tokens)
            total = total + jnp.dot(ref[e, mine, :], back_ref[rows, :], preferred_element_type=jnp.float32)
        out_ref[...] = total


def weight_halves(core, order, pair, from_right, far, from_left, back_all, step):
    features, tokens = pair.shape[1:]
    width = back_all.shape[1]
    fixed = lambda size: pl.BlockSpec((size, features, tokens), lambda j, plan_ref: (0, 0, 0))
    columns = lambda rows: pl.BlockSpec((rows, step), lambda j, plan_ref: (0, j))
    return pl.pallas_call(
        weight_kernel,
        grid_spec=pltpu.PrefetchScalarGridSpec(
            num_scalar_prefetch=1,
            grid=(width // step,),
            in_specs=[fixed(2), fixed(2), fixed(1), fixed(1), fixed(2), columns(back_all.shape[0])],
            out_specs=[columns(features // 2)] * 2,
        ),
        out_shape=[jax.ShapeDtypeStruct((features // 2, width), jnp.float32)] * 2,
        compiler_params=pltpu.CompilerParams(vmem_limit_bytes=56 * 2**20),
    )(jnp.stack([core, *order]).astype(jnp.int32), pair, from_right, *far, from_left, back_all)


def add_kernel(mine_ref, other_ref, query_ref, key_ref, value_ref):
    total = mine_ref[...] + other_ref[...]
    query_width, key_width = query_ref.shape[1], key_ref.shape[1]
    query_ref[...] = total[:, :query_width]
    key_ref[...] = total[:, query_width : query_width + key_width]
    value_ref[...] = total[:, query_width + key_width :]


def summed_columns(mine, other, widths):
    rows, width = mine.shape
    step = rows // 4
    block = lambda w: pl.BlockSpec((step, w), lambda i: (i, 0))
    return pl.pallas_call(
        add_kernel,
        grid=(rows // step,),
        in_specs=[block(width)] * 2,
        out_specs=[block(w) for w in widths],
        out_shape=[jax.ShapeDtypeStruct((rows, w), mine.dtype) for w in widths],
    )(mine, other)


def shifted(values, axis, by):
    size = lax.axis_size(axis)
    return lax.ppermute(values, axis, [(i, (i + by) % size) for i in range(size)])


def to_feature_owner(values, lows, depth, cores, ring, highs):
    place = lambda y_lo, z, core, x, y_hi: (((y_lo * depth + z) * cores + core) * ring + x) * highs + y_hi
    pairs = []
    for y_lo, z, core, x, y_hi in itertools.product(range(lows), range(depth), range(cores), range(ring), range(highs)):
        owner = x * highs + y_hi
        target = (owner // depth, owner % depth, core, (z + x) % ring, y_lo ^ y_hi ^ (x // 2))
        pairs.append((place(y_lo, z, core, x, y_hi), place(*target)))
    return lax.ppermute(values, DP + TENSOR, pairs)


def body(normed, query_back, key_back, value_back, query_proj, key_proj, value_proj, source):
    y_lo, z, core = (lax.axis_index(a) for a in DP)
    x, y_hi = (lax.axis_index(a) for a in TENSOR)
    lows, depth, cores = (lax.axis_size(a) for a in DP)
    ring, highs = (lax.axis_size(a) for a in TENSOR)
    dp_count, groups = lows * depth * cores, ring * highs
    my_index = (y_lo * depth + z) * cores + core
    capacity, features = normed.shape
    per_pair = capacity // dp_count
    tokens = source.shape[0] // dp_count
    query_width, key_width = query_back.shape[1], key_back.shape[1]
    width = query_width + 2 * key_width
    flat_slots = balanced_slots(source, dp_count, per_pair)

    packed = pack_rows(source, my_index, dp_count, per_pair, (normed, query_back, key_back, value_back))
    packed = packed.reshape(dp_count, per_pair, -1)
    relayed = lax.all_to_all(packed, DP, split_axis=0, concat_axis=0, tiled=True).reshape(capacity, -1)
    back_mine = take_rows(relayed[:, features:], flat_slots)

    inputs_mine = take_rows_across(relayed[:, :features], flat_slots)
    inputs_mine = to_feature_owner(inputs_mine, lows, depth, cores, ring, highs)

    projections = (query_proj, key_proj, value_proj)
    block_at = lambda offsets, y: jnp.stack([(x + s) % ring * highs + y for s in offsets]).astype(jnp.int32)
    away = (2, 1, ring - 1)
    part_of = functools.partial(partials, rows=back_mine, projections=projections, features=features)
    near = part_of(block_at(away + (0,), 1 - y_hi), (len(away), 1))
    other_back = shifted(back_mine, "y_lo", 1)
    inputs_mine, other_back, near = lax.optimization_barrier((inputs_mine, other_back, near))
    copies = jnp.broadcast_to(jnp.stack([back_mine, other_back])[None], (depth, lows) + back_mine.shape)
    inputs_near = shifted(inputs_mine, "y_hi", 1)
    inputs_near, copies, near = lax.optimization_barrier((inputs_near, copies, near))
    pair = jnp.stack([inputs_mine, inputs_near])
    near_away, near_here = [shifted(block, "y_hi", 1) for block in near]
    back_all = lax.all_to_all(copies, "z", split_axis=0, concat_axis=0, tiled=True).reshape(-1, width)
    source_x = y_lo * (depth // highs) + z // highs
    turned = (y_hi + z) % lows
    order = [(x + s - source_x) % depth * lows + (turned + e) % lows for s in range(ring) for e in range(highs)]

    from_left, from_right = shifted(pair, "x", 1), shifted(pair, "x", -1)
    places = jnp.stack([(x + s) % ring for s in away]).astype(jnp.int32)
    (to_others,) = part_of(
        block_at(away, y_hi), (len(away),), arrived=((near_away, jnp.arange(len(away))),), places=places
    )
    far = [shifted(from_left[:1], "x", 1), shifted(from_right[1:], "x", -1)]
    from_others = lax.all_to_all(to_others, "x", split_axis=0, concat_axis=0, tiled=True)
    far, near_here, _ = lax.optimization_barrier((far, near_here, to_others))

    for_other, weight_grad = weight_halves(core, order, pair, from_right, far, from_left, back_all, 2 * key_width)
    from_other = shifted(for_other, "core", 1)
    grads = summed_columns(weight_grad, from_other, (query_width, key_width, key_width))
    (here,) = part_of(block_at((0,), y_hi), (1,), arrived=((near_here, jnp.zeros(1)),), coded_out=False)
    return *grads, decoded_sum(here[0], from_others, places)


def solution(mesh):
    shape = [size for _, size in DP_SIZES + TENSOR_SIZES]
    by_chip = Mesh(mesh.devices.reshape(shape), DP + TENSOR)
    in_specs = (
        P(DP, TENSOR),
        P(DP, TENSOR),
        P(DP, TENSOR),
        P(DP, TENSOR),
        P(None, TENSOR),
        P(None, TENSOR),
        P(None, TENSOR),
        P(),
    )
    out_specs = (P(DP, TENSOR), P(DP, TENSOR), P(DP, TENSOR), P(DP, TENSOR))
    return jax.shard_map(body, mesh=by_chip, in_specs=in_specs, out_specs=out_specs, check_vma=False)
```

profile of v0, /device:TPU:24, one launch (start us, length us, event | category | flops | bytes accessed | tf_op | source)
XLA Modules:
  0.0 163.9 jit_solution(5300335233520662302)
XLA Ops:
  2.0 4.4 %shard_map.111 = bf16[512,1792]{1,0:T(8,128)(2,1)} custom-call(s32[1]{0:T(128)} %bitcast.9.me_ref, s32[16,256]{1,0:T(8,128)} %reshape.28.slots_ref, bf16[512,1024]{1,0:T(8,128)(2,1)} %refs_0_.1, bf16[512,512]{1,0:T(8,128)(2,1)} %refs_1_.1, bf16[512,128]{1,0:T(8,128)(2,1)} %refs_2_.1, bf16[512,128]{1,0:T(8,128)(2,1)} %refs_3_.1), custom_call_target="tpu_custom_call" | custom-call | tf_op jit(solution)/shard_map/pallas_call | solution.py:61
  6.3 6.8 %all-to-all-start = ((bf16[16,32,1792]{2,1,0:T(8,128)(2,1)}), bf16[16,32,1792]{2,1,0:T(8,128)(2,1)S(1)}, u32[]{:S(2)}, u32[]{:S(2)}) async-start(bf16[16,32,1792]{2,1,0:T(8,128)(2,1)} %bitcast.30), calls=%async_computation | async-start | bytes 3670016 | tf_op jit(solution)/shard_map/all_to_all | solution.py:276
  14.7 22.5 %all-to-all-done = bf16[16,32,1792]{2,1,0:T(8,128)(2,1)S(1)} async-done(((bf16[16,32,1792]{2,1,0:T(8,128)(2,1)}), bf16[16,32,1792]{2,1,0:T(8,128)(2,1)S(1)}, u32[]{:S(2)}, u32[]{:S(2)}) %all-to-all-start) | async-done | bytes 1835040 | tf_op jit(solution)/shard_map/all_to_all | solution.py:276
  37.8 2.7 %collective-permute-start = (bf16[1024,256]{1,0:T(8,128)(2,1)S(1)}, bf16[1024,256]{1,0:T(8,128)(2,1)S(1)}, u32[]{:S(2)}, u32[]{:S(2)}) collective-permute-start(bf16[1024,256]{1,0:T(8,128)(2,1)S(1)} %convolution_convert_fusion), channel_id=1, source_target_pairs={{0,0},{1,17},{2,34},{3,51},{4,69},{5,84},{6,103},{7,118},{8,8},{9,... | collective-permute-start | bytes 1572872 | tf_op jit(solution)/shard_map/ppermute | solution.py:257
  42.5 7.5 %shard_map.112 = (s16[3,272,1024]{2,1,0:T(8,128)(2,1)}, s16[1,272,1024]{2,1,0:T(8,128)(2,1)}) custom-call(s32[4]{0:T(128)} %pad_add_fusion.order_ref, bf16[256,768]{1,0:T(8,128)(2,1)} %copy-done.2, bf16[8192,512]{1,0:T(8,128)(2,1)} %query_ref.5, bf16[8192,128]{1,0:T(8,128)(2,1)} %key_ref.5, bf16[8192,128]{1,0:T(8,128)(2,1)} %value_ref.5), custom_call_target="tpu_custom_call" | custom-call | tf_op jit(solution)/shard_map/pallas_call | solution.py:146
  51.3 7.8 %collective-permute-done = bf16[1024,256]{1,0:T(8,128)(2,1)S(1)} collective-permute-done((bf16[1024,256]{1,0:T(8,128)(2,1)S(1)}, bf16[1024,256]{1,0:T(8,128)(2,1)S(1)}, u32[]{:S(2)}, u32[]{:S(2)}) %collective-permute-start) | collective-permute-done | bytes 524320 | tf_op jit(solution)/shard_map/ppermute | solution.py:257
  60.4 12.9 %collective-permute-done.2 = bf16[1024,256]{1,0:T(8,128)(2,1)} collective-permute-done((bf16[1024,256]{1,0:T(8,128)(2,1)S(1)}, bf16[1024,256]{1,0:T(8,128)(2,1)}, u32[]{:S(2)}, u32[]{:S(2)}) %collective-permute-start.2) | collective-permute-done | bytes 524320 | tf_op jit(solution)/shard_map/ppermute | solution.py:247
  73.3 1.8 %broadcast_in_dim.2 = bf16[4,2,256,768]{3,2,1,0:T(8,128)(2,1)} broadcast(bf16[2,256,768]{2,1,0:T(8,128)(2,1)S(1)} %pad_maximum_fusion.1), dimensions={1,2,3} | broadcast | bytes 3932160 | tf_op jit(solution)/shard_map/broadcast_in_dim | solution.py:289
  75.2 3.8 %all-to-all-start.1 = ((bf16[4,2,256,768]{3,2,1,0:T(8,128)(2,1)}), bf16[4,2,256,768]{3,2,1,0:T(8,128)(2,1)S(1)}, u32[]{:S(2)}, u32[]{:S(2)}) async-start(bf16[4,2,256,768]{3,2,1,0:T(8,128)(2,1)} %broadcast_in_dim.2), calls=%async_computation.1 | async-start | bytes 6291456 | tf_op jit(solution)/shard_map/all_to_all | solution.py:294
  79.0 2.1 %collective-permute-start.8 = (s16[3,272,1024]{2,1,0:T(8,128)(2,1)}, s16[3,272,1024]{2,1,0:T(8,128)(2,1)}, u32[]{:S(2)}, u32[]{:S(2)}) collective-permute-start(s16[3,272,1024]{2,1,0:T(8,128)(2,1)} %get-tuple-element.30), channel_id=1, source_target_pairs={{0,1},{1,0},{2,3},{3,2},{4,5},{5,4},{6,7},{7,6},{8,9},{9,8},{10,11... | collective-permute-start | bytes 5013512 | tf_op jit(solution)/shard_map/ppermute | solution.py:247
  83.4 2.3 %collective-permute-start.3 = (bf16[2,1024,256]{2,1,0:T(8,128)(2,1)S(1)}, bf16[2,1024,256]{2,1,0:T(8,128)(2,1)S(1)}, u32[]{:S(2)}, u32[]{:S(2)}) collective-permute-start(bf16[2,1024,256]{2,1,0:T(8,128)(2,1)S(1)} %pad_maximum_fusion.pair_ref), channel_id=1, source_target_pairs={{0,6},{2,0},{4,2},{6,4},{1,7},{3,1},{5,3},{7,5},{8,14},{10,8},{12,... | collective-permute-start | bytes 3145736 | tf_op jit(solution)/shard_map/ppermute | solution.py:247
  85.7 1.4 collective-permute-start.7
  87.1 19.6 %collective-permute-done.4.left_ref = bf16[2,1024,256]{2,1,0:T(8,128)(2,1)S(1)} collective-permute-done((bf16[2,1024,256]{2,1,0:T(8,128)(2,1)S(1)}, bf16[2,1024,256]{2,1,0:T(8,128)(2,1)S(1)}, u32[]{:S(2)}, u32[]{:S(2)}) %collective-permute-start.4) | collective-permute-done | bytes 1048608 | tf_op jit(solution)/shard_map/ppermute | solution.py:247
  109.1 3.0 %collective-permute-start.6 = (bf16[1,1024,256]{2,1,0:T(8,128)(2,1)}, bf16[1,1024,256]{2,1,0:T(8,128)(2,1)}, u32[]{:S(2)}, u32[]{:S(2)}) collective-permute-start(bf16[1,1024,256]{2,1,0:T(8,128)(2,1)} %slice.23), channel_id=1, source_target_pairs={{0,6},{2,0},{4,2},{6,4},{1,7},{3,1},{5,3},{7,5},{8,14},{10,8},{12,... | collective-permute-start | bytes 1572872 | tf_op jit(solution)/shard_map/ppermute | solution.py:247
  112.8 7.5 %collective-permute-done.8.refs_0_ = s16[3,272,1024]{2,1,0:T(8,128)(2,1)} collective-permute-done((s16[3,272,1024]{2,1,0:T(8,128)(2,1)}, s16[3,272,1024]{2,1,0:T(8,128)(2,1)}, u32[]{:S(2)}, u32[]{:S(2)}) %collective-permute-start.8) | collective-permute-done | bytes 1671200 | tf_op jit(solution)/shard_map/ppermute | solution.py:247
  120.2 6.7 %shard_map.113 = s16[4,272,1024]{2,1,0:T(8,128)(2,1)} custom-call(s32[9]{0:T(128)} %concatenate.7.order_ref, bf16[256,768]{1,0:T(8,128)(2,1)} %copy-done.2, bf16[8192,512]{1,0:T(8,128)(2,1)} %query_ref.5, bf16[8192,128]{1,0:T(8,128)(2,1)} %key_ref.5, bf16[8192,128]{1,0:T(8,128)(2,1)} %value_ref.5, s16[3,272,1024]{2,1,0:T(8,128)(2,1)} %collective-permute-done.8.refs_0_), custom_call_target="tpu_custom_call" | custom-call | tf_op jit(solution)/shard_map/pallas_call | solution.py:146
  127.0 1.6 copy-done.1
  128.6 3.6 %all-to-all-start.2 = ((s16[4,272,1024]{2,1,0:T(8,128)(2,1)}), s16[4,272,1024]{2,1,0:T(8,128)(2,1)S(1)}, u32[]{:S(2)}, u32[]{:S(2)}) async-start(s16[4,272,1024]{2,1,0:T(8,128)(2,1)} %shard_map.113), calls=%async_computation.2 | async-start | bytes 4456448 | tf_op jit(solution)/shard_map/all_to_all | solution.py:305
  132.9 8.4 %shard_map.114 = (f32[512,768]{1,0:T(8,128)}, f32[512,768]{1,0:T(8,128)}) custom-call(s32[9]{0:T(128)} %stack.96.plan_ref, bf16[2,1024,256]{2,1,0:T(8,128)(2,1)} %copy-done.3, bf16[2,1024,256]{2,1,0:T(8,128)(2,1)} %copy-done.5, bf16[1,1024,256]{2,1,0:T(8,128)(2,1)} %collective-permute-done.5.far_0_ref, ...), custom_call_target="tpu_custom_call" | custom-call | tf_op jit(solution)/shard_map/pallas_call | solution.py:211
  142.5 3.9 %shard_map.116 = f32[1,256,1024]{2,1,0:T(8,128)} custom-call(s32[2]{0:T(128)} %pad_add_fusion.2.order_ref, bf16[256,768]{1,0:T(8,128)(2,1)} %copy-done.2, bf16[8192,512]{1,0:T(8,128)(2,1)} %query_ref.5, bf16[8192,128]{1,0:T(8,128)(2,1)} %key_ref.5, bf16[8192,128]{1,0:T(8,128)(2,1)} %value_ref.5, s16[1,272,1024]{2,1,0:T(8,128)(2,1)} %collective-permute-done.7.refs_0_), custom_call_target="tpu_custom_call" | custom-call | tf_op jit(solution)/shard_map/pallas_call | solution.py:146
  146.4 8.6 %all-to-all-done.2.refs_0_.refs_1_.refs_2_.refs_3_.refs_4_.refs_5_ = s16[4,272,1024]{2,1,0:T(8,128)(2,1)S(1)} async-done(((s16[4,272,1024]{2,1,0:T(8,128)(2,1)}), s16[4,272,1024]{2,1,0:T(8,128)(2,1)S(1)}, u32[]{:S(2)}, u32[]{:S(2)}) %all-to-all-start.2) | async-done | bytes 2228256 | tf_op jit(solution)/shard_map/all_to_all | solution.py:305
  155.0 1.4 copy-done
  156.4 3.6 %shard_map.117 = f32[256,1024]{1,0:T(8,128)} custom-call(s32[3]{0:T(128)} %pad_add_fusion.1.plan_ref, f32[256,1024]{1,0:T(8,128)} %bitcast.32, s16[4,272,1024]{2,1,0:T(8,128)(2,1)} %copy-done, s16[4,272,1024]{2,1,0:T(8,128)(2,1)} %copy-done, s16[4,272,1024]{2,1,0:T(8,128)(2,1)} %copy-done, s16[4,272,1024]{2,1,0:T(8,128)(2,1)} %copy-done, ...), custom_call_target="tpu_custom_call" | custom-call | tf_op jit(solution)/shard_map/pallas_call | solution.py:183
  160.0 3.9 %shard_map.115 = (f32[512,512]{1,0:T(8,128)}, f32[512,128]{1,0:T(8,128)}, f32[512,128]{1,0:T(8,128)}) custom-call(f32[512,768]{1,0:T(8,128)} %get-tuple-element.34.mine_ref, f32[512,768]{1,0:T(8,128)} %collective-permute-done.9.other_ref), custom_call_target="tpu_custom_call" | custom-call | tf_op jit(solution)/shard_map/pallas_call | solution.py:236
  (40 shorter events, 15.2 us)
Async XLA Ops:
  6.3 30.9 %all-to-all-start = ((bf16[16,32,1792]{2,1,0:T(8,128)(2,1)}), bf16[16,32,1792]{2,1,0:T(8,128)(2,1)S(1)}, u32[]{:S(2)}, u32[]{:S(2)}) async-start(bf16[16,32,1792]{2,1,0:T(8,128)(2,1)} %bitcast.30), calls=%async_computation | async-start | bytes 3670016 | tf_op jit(solution)/shard_map/all_to_all | solution.py:276
  37.8 21.4 %collective-permute-start = (bf16[1024,256]{1,0:T(8,128)(2,1)S(1)}, bf16[1024,256]{1,0:T(8,128)(2,1)S(1)}, u32[]{:S(2)}, u32[]{:S(2)}) collective-permute-start(bf16[1024,256]{1,0:T(8,128)(2,1)S(1)} %convolution_convert_fusion), channel_id=1, source_target_pairs={{0,0},{1,17},{2,34},{3,51},{4,69},{5,84},{6,103},{7,118},{8,8},{9,... | collective-permute-start | bytes 1572872 | tf_op jit(solution)/shard_map/ppermute | solution.py:257
  40.8 1.7 %copy-start.2 = (bf16[256,768]{1,0:T(8,128)(2,1)}, bf16[256,768]{1,0:T(8,128)(2,1)S(1)}, u32[]{:S(2)}) copy-start(bf16[256,768]{1,0:T(8,128)(2,1)S(1)} %convolution_convert_fusion.1.rows_ref) | copy-start | bytes 1179652
  40.8 10.5 %collective-permute-start.1 = (bf16[256,768]{1,0:T(8,128)(2,1)S(1)}, bf16[256,768]{1,0:T(8,128)(2,1)S(1)}, u32[]{:S(2)}, u32[]{:S(2)}) collective-permute-start(bf16[256,768]{1,0:T(8,128)(2,1)S(1)} %convolution_convert_fusion.1.rows_ref), channel_id=1, source_target_pairs={{0,64},{64,0},{1,65},{65,1},{2,66},{66,2},{3,67},{67,3},{4,68},{68... | collective-permute-start | bytes 1179656 | tf_op jit(solution)/shard_map/ppermute | solution.py:247
  59.1 16.0 %copy-start.6 = (bf16[1024,256]{1,0:T(8,128)(2,1)}, bf16[1024,256]{1,0:T(8,128)(2,1)S(1)}, u32[]{:S(2)}) copy-start(bf16[1024,256]{1,0:T(8,128)(2,1)S(1)} %collective-permute-done) | copy-start | bytes 1572868
  59.1 14.2 %collective-permute-start.2 = (bf16[1024,256]{1,0:T(8,128)(2,1)S(1)}, bf16[1024,256]{1,0:T(8,128)(2,1)}, u32[]{:S(2)}, u32[]{:S(2)}) collective-permute-start(bf16[1024,256]{1,0:T(8,128)(2,1)S(1)} %collective-permute-done), channel_id=1, source_target_pairs={{0,1},{1,0},{2,3},{3,2},{4,5},{5,4},{6,7},{7,6},{8,9},{9,8},{10,11... | collective-permute-start | bytes 1572872 | tf_op jit(solution)/shard_map/ppermute | solution.py:247
  75.2 51.8 %all-to-all-start.1 = ((bf16[4,2,256,768]{3,2,1,0:T(8,128)(2,1)}), bf16[4,2,256,768]{3,2,1,0:T(8,128)(2,1)S(1)}, u32[]{:S(2)}, u32[]{:S(2)}) async-start(bf16[4,2,256,768]{3,2,1,0:T(8,128)(2,1)} %broadcast_in_dim.2), calls=%async_computation.1 | async-start | bytes 6291456 | tf_op jit(solution)/shard_map/all_to_all | solution.py:294
  79.0 41.3 %collective-permute-start.8 = (s16[3,272,1024]{2,1,0:T(8,128)(2,1)}, s16[3,272,1024]{2,1,0:T(8,128)(2,1)}, u32[]{:S(2)}, u32[]{:S(2)}) collective-permute-start(s16[3,272,1024]{2,1,0:T(8,128)(2,1)} %get-tuple-element.30), channel_id=1, source_target_pairs={{0,1},{1,0},{2,3},{3,2},{4,5},{5,4},{6,7},{7,6},{8,9},{9,8},{10,11... | collective-permute-start | bytes 5013512 | tf_op jit(solution)/shard_map/ppermute | solution.py:247
  82.4 1.0 copy-start.3
  82.4 24.4 %collective-permute-start.4 = (bf16[2,1024,256]{2,1,0:T(8,128)(2,1)S(1)}, bf16[2,1024,256]{2,1,0:T(8,128)(2,1)S(1)}, u32[]{:S(2)}, u32[]{:S(2)}) collective-permute-start(bf16[2,1024,256]{2,1,0:T(8,128)(2,1)S(1)} %pad_maximum_fusion.pair_ref), channel_id=1, source_target_pairs={{0,2},{2,4},{4,6},{6,0},{1,3},{3,5},{5,7},{7,1},{8,10},{10,12},{12... | collective-permute-start | bytes 3145736 | tf_op jit(solution)/shard_map/ppermute | solution.py:247
  83.4 24.3 %collective-permute-start.3 = (bf16[2,1024,256]{2,1,0:T(8,128)(2,1)S(1)}, bf16[2,1024,256]{2,1,0:T(8,128)(2,1)S(1)}, u32[]{:S(2)}, u32[]{:S(2)}) collective-permute-start(bf16[2,1024,256]{2,1,0:T(8,128)(2,1)S(1)} %pad_maximum_fusion.pair_ref), channel_id=1, source_target_pairs={{0,6},{2,0},{4,2},{6,4},{1,7},{3,1},{5,3},{7,5},{8,14},{10,8},{12,... | collective-permute-start | bytes 3145736 | tf_op jit(solution)/shard_map/ppermute | solution.py:247
  85.7 47.2 %collective-permute-start.7 = (s16[1,272,1024]{2,1,0:T(8,128)(2,1)}, s16[1,272,1024]{2,1,0:T(8,128)(2,1)}, u32[]{:S(2)}, u32[]{:S(2)}) collective-permute-start(s16[1,272,1024]{2,1,0:T(8,128)(2,1)} %get-tuple-element.29), channel_id=1, source_target_pairs={{0,1},{1,0},{2,3},{3,2},{4,5},{5,4},{6,7},{7,6},{8,9},{9,8},{10,11... | collective-permute-start | bytes 1671176 | tf_op jit(solution)/shard_map/ppermute | solution.py:247
  106.8 1.2 copy-start.4
  107.7 25.2 %collective-permute-start.5 = (bf16[1,1024,256]{2,1,0:T(8,128)(2,1)}, bf16[1,1024,256]{2,1,0:T(8,128)(2,1)}, u32[]{:S(2)}, u32[]{:S(2)}) collective-permute-start(bf16[1,1024,256]{2,1,0:T(8,128)(2,1)} %slice.22), channel_id=1, source_target_pairs={{0,2},{2,4},{4,6},{6,0},{1,3},{3,5},{5,7},{7,1},{8,10},{10,12},{12... | collective-permute-start | bytes 1572872 | tf_op jit(solution)/shard_map/ppermute | solution.py:247
  107.9 1.1 copy-start.5
  109.1 23.9 %collective-permute-start.6 = (bf16[1,1024,256]{2,1,0:T(8,128)(2,1)}, bf16[1,1024,256]{2,1,0:T(8,128)(2,1)}, u32[]{:S(2)}, u32[]{:S(2)}) collective-permute-start(bf16[1,1024,256]{2,1,0:T(8,128)(2,1)} %slice.23), channel_id=1, source_target_pairs={{0,6},{2,0},{4,2},{6,4},{1,7},{3,1},{5,3},{7,5},{8,14},{10,8},{12,... | collective-permute-start | bytes 1572872 | tf_op jit(solution)/shard_map/ppermute | solution.py:247
  126.9 1.6 %copy-start.1 = (bf16[4,2,256,768]{3,2,1,0:T(8,128)(2,1)}, bf16[4,2,256,768]{3,2,1,0:T(8,128)(2,1)S(1)}, u32[]{:S(2)}) copy-start(bf16[4,2,256,768]{3,2,1,0:T(8,128)(2,1)S(1)} %all-to-all-done.1) | copy-start | bytes 9437188
  128.6 26.4 %all-to-all-start.2 = ((s16[4,272,1024]{2,1,0:T(8,128)(2,1)}), s16[4,272,1024]{2,1,0:T(8,128)(2,1)S(1)}, u32[]{:S(2)}, u32[]{:S(2)}) async-start(s16[4,272,1024]{2,1,0:T(8,128)(2,1)} %shard_map.113), calls=%async_computation.2 | async-start | bytes 4456448 | tf_op jit(solution)/shard_map/all_to_all | solution.py:305
  141.4 18.7 %collective-permute-start.9 = (f32[512,768]{1,0:T(8,128)}, f32[512,768]{1,0:T(8,128)}, u32[]{:S(2)}, u32[]{:S(2)}) collective-permute-start(f32[512,768]{1,0:T(8,128)} %get-tuple-element.35), channel_id=1, source_target_pairs={{0,8},{8,0},{1,9},{9,1},{2,10},{10,2},{3,11},{11,3},{4,12},{12,4},... | collective-permute-start | bytes 4718600 | tf_op jit(solution)/shard_map/ppermute | solution.py:247
  155.0 1.4 copy-start
where the time goes:
time: 167 us; the launch traced here: 164 us
  waiting for transfers between devices  80.2 us (48%)
  Pallas kernels  38.4 us (23%)
  starting transfers between devices  27.1 us (16%)
  local copies, waits for them, and re-layouts  10.4 us (6%)
  other arithmetic  5.95 us (4%)
    ppermute x9, waiting for transfers between devices, shifted(): lax.ppermute(values, axis, [(i, (i + by) % size) for i in range(size)])  41.3 us
    all_to_all x1, waiting for transfers between devices, body(): lax.all_to_all(packed, DP, split_axis=0, concat_axis=0, tiled=True)  22.5 us
    pallas_call x3, Pallas kernels, partials(): pl.pallas_call(functools.partial(partial_kernel, sizes, len(arrived), cod...  18.1 us
    ppermute x9, starting transfers between devices, shifted(): lax.ppermute(values, axis, [(i, (i + by) % size) for i in range(size)])  10.2 us
    all_to_all x1, waiting for transfers between devices, body(): lax.all_to_all(to_others, 'x', split_axis=0, concat_axis=0, tiled=True)  8.56 us
    pallas_call x1, Pallas kernels, weight_halves(): pl.pallas_call(weight_kernel, grid_spec=pltpu.PrefetchScalarGridSpec(num_...  8.42 us
    ppermute x1, waiting for transfers between devices, to_feature_owner(): return lax.ppermute(values, DP + TENSOR, pairs)  7.84 us
    all_to_all x1, starting transfers between devices, body(): lax.all_to_all(packed, DP, split_axis=0, concat_axis=0, tiled=True)  6.79 us
  transfers between devices with their start and end apart: 13, of which 7 were waited for; matrix products, arithmetic and copies ran while one was open for 6% of the time, Pallas kernels for 18%

commit v1 on v0

--- a/solution.py
+++ b/solution.py
@@ -67,7 +67,7 @@
             out_specs=whole((capacity, width)),
         ),
         out_shape=jax.ShapeDtypeStruct((capacity, width), values[0].dtype),
-        compiler_params=pltpu.CompilerParams(vmem_limit_bytes=60 * 2**20),
+        compiler_params=pltpu.CompilerParams(vmem_limit_bytes=62 * 2**20),
     )(my_index.reshape(1), slots, *values)
 
 
@@ -84,6 +84,22 @@
 
 def column_of(row_values, tokens):
     return jnp.transpose(jnp.broadcast_to(row_values, (128, tokens)))[:, :1]
+
+
+def decoded(coded, exponent, tokens):
+    step = jnp.exp2(column_of(exponent.astype(jnp.int32).astype(jnp.float32)[:1], tokens) - FRACTION_BITS)
+    return coded.astype(jnp.int32).astype(jnp.float32) * step
+
+
+def encoded(part):
+    tokens, width = part.shape
+    most = jnp.max(jnp.abs(part), axis=1, keepdims=True)
+    exponent = jnp.floor(jnp.log2(jnp.maximum(most, 2.0**-100))) + 1.0
+    coded = jnp.round(part * jnp.exp2(FRACTION_BITS - exponent))
+    coded = jnp.clip(coded, -32767.0, 32767.0).astype(jnp.int32).astype(jnp.int16)
+    across = jnp.transpose(jnp.broadcast_to(exponent, (tokens, 128)))[:SCALE_ROWS, :]
+    across = jnp.concatenate([across, jnp.zeros((SCALE_ROWS, width - tokens), jnp.float32)], axis=1)
+    return coded, across.astype(jnp.int32).astype(jnp.int16)
 
 
 def partial_kernel(sizes, arrivals, coded_out, order_ref, rows_ref, query_ref, key_ref, value_ref, *refs):
@@ -99,20 +115,11 @@
         rows_ref[:, query_width:], others, contract, preferred_element_type=jnp.float32
     )
     for ref in refs[:arrivals]:
-        exponent = ref[0, tokens:, :tokens].astype(jnp.int32).astype(jnp.float32)[:1]
-        step = jnp.exp2(column_of(exponent, tokens) - FRACTION_BITS)
-        part = part + ref[0, :tokens, :].astype(jnp.int32).astype(jnp.float32) * step
+        part = part + decoded(ref[0, :tokens, :], ref[0, tokens:, :tokens], tokens)
     if not coded_out:
         refs[-1][0] = part
         return
-    most = jnp.max(jnp.abs(part), axis=1, keepdims=True)
-    exponent = jnp.floor(jnp.log2(jnp.maximum(most, 2.0**-100))) + 1.0
-    coded = jnp.round(part * jnp.exp2(FRACTION_BITS - exponent))
-    coded = jnp.clip(coded, -32767.0, 32767.0).astype(jnp.int32).astype(jnp.int16)
-    across = jnp.transpose(jnp.broadcast_to(exponent, (tokens, 128)))[:SCALE_ROWS, :]
-    width = coded.shape[1]
-    across = jnp.concatenate([across, jnp.zeros((SCALE_ROWS, width - tokens), jnp.float32)], axis=1)
-    across = across.astype(jnp.int32).astype(jnp.int16)
+    coded, across = encoded(part)
     first = 0
     for size, out_ref in zip(sizes, refs[arrivals:]):
 
@@ -124,38 +131,52 @@
         first += size
 
 
-def partials(order, sizes, rows, projections, features, arrived=(), places=None, coded_out=True):
+def partials(order, sizes, rows, projections, features, arrived=(), coded_out=True):
     tokens, width = rows.shape
-    steps = sum(sizes)
     coded_block = (1, tokens + SCALE_ROWS, features)
     out_block = coded_block if coded_out else (1, tokens, features)
     kind = jnp.int16 if coded_out else jnp.float32
-    plan = [order]
-    column = lambda values: plan.append(values.astype(jnp.int32)) or len(plan) - 1
-    chosen = lambda g, plan_ref: (plan_ref[g], 0)
-    in_turn = lambda first, size: lambda g, plan_ref: (jnp.clip(g - first, 0, size - 1), 0, 0)
-    listed = lambda at: lambda g, plan_ref: (plan_ref[at * steps + g], 0, 0)
-    arrived_specs = [pl.BlockSpec(coded_block, listed(column(blocks))) for _, blocks in arrived]
-    if places is None:
-        firsts = [sum(sizes[:i]) for i in range(len(sizes))]
-        out_specs = [pl.BlockSpec(out_block, in_turn(f, n)) for f, n in zip(firsts, sizes)]
-        out_counts = sizes
-    else:
-        out_specs = [pl.BlockSpec(out_block, listed(column(places)))]
-        out_counts = (places.shape[0] + 1,)
+    chosen = lambda g, order_ref: (order_ref[g], 0)
+    in_turn = lambda first, size: lambda g, order_ref: (jnp.clip(g - first, 0, size - 1), 0, 0)
+    firsts = [sum(sizes[:i]) for i in range(len(sizes))]
     return pl.pallas_call(
         functools.partial(partial_kernel, sizes, len(arrived), coded_out),
         grid_spec=pltpu.PrefetchScalarGridSpec(
             num_scalar_prefetch=1,
-            grid=(steps,),
-            in_specs=[pl.BlockSpec((tokens, width), lambda g, plan_ref: (0, 0))]
+            grid=(sum(sizes),),
+            in_specs=[pl.BlockSpec((tokens, width), lambda g, order_ref: (0, 0))]
             + [pl.BlockSpec((features, p.shape[1]), chosen) for p in projections]
-            + arrived_specs,
-            out_specs=out_specs,
-        ),
-        out_shape=[jax.ShapeDtypeStruct((n,) + out_block[1:], kind) for n in out_counts],
+            + [pl.BlockSpec(coded_block, lambda g, order_ref: (g, 0, 0)) for _ in arrived],
+            out_specs=[pl.BlockSpec(out_block, in_turn(f, n)) for f, n in zip(firsts, sizes)],
+        ),
+        out_shape=[jax.ShapeDtypeStruct((n,) + out_block[1:], kind) for n in sizes],
         compiler_params=pltpu.CompilerParams(vmem_limit_bytes=56 * 2**20),
-    )(jnp.concatenate(plan), rows, *projections, *(values for values, _ in arrived))
+    )(order, rows, *projections, *arrived)
+
+
+def recode_kernel(places_ref, own_ref, near_ref, out_ref):
+    tokens = own_ref.shape[1]
+    part = own_ref[0] + decoded(near_ref[0, :tokens, :], near_ref[0, tokens:, :tokens], tokens)
+    out_ref[0, :tokens, :], out_ref[0, tokens:, :] = encoded(part)
+
+
+def recoded(own, near, places):
+    blocks, tokens, features = own.shape
+    coded_block = (1, tokens + SCALE_ROWS, features)
+    return pl.pallas_call(
+        recode_kernel,
+        grid_spec=pltpu.PrefetchScalarGridSpec(
+            num_scalar_prefetch=1,
+            grid=(blocks,),
+            in_specs=[
+                pl.BlockSpec((1, tokens, features), lambda g, places_ref: (g, 0, 0)),
+                pl.BlockSpec(coded_block, lambda g, places_ref: (g, 0, 0)),
+            ],
+            out_specs=pl.BlockSpec(coded_block, lambda g, places_ref: (places_ref[g], 0, 0)),
+        ),
+        out_shape=jax.ShapeDtypeStruct((blocks + 1,) + coded_block[1:], jnp.int16),
+        compiler_params=pltpu.CompilerParams(vmem_limit_bytes=56 * 2**20),
+    )(places, own, near)
 
 
 def sum_kernel(plan_ref, here_ref, *refs):
@@ -163,9 +184,7 @@
     tokens = here_ref.shape[0]
     total = here_ref[...]
     for exponent_ref, coded_ref in zip(refs[:-1:2], refs[1:-1:2]):
-        exponent = exponent_ref[0].astype(jnp.int32).astype(jnp.float32)[:1]
-        step = jnp.exp2(column_of(exponent, tokens) - FRACTION_BITS)
-        total = total + coded_ref[0].astype(jnp.int32).astype(jnp.float32) * step
+        total = total + decoded(coded_ref[0], exponent_ref[0], tokens)
     out_ref[...] = total
 
 
@@ -186,7 +205,7 @@
             num_scalar_prefetch=1, grid=(features // step,), in_specs=in_specs, out_specs=columns
         ),
         out_shape=jax.ShapeDtypeStruct((tokens, features), jnp.float32),
-        compiler_params=pltpu.CompilerParams(vmem_limit_bytes=60 * 2**20),
+        compiler_params=pltpu.CompilerParams(vmem_limit_bytes=62 * 2**20),
     )(places, *operands)
 
 
@@ -217,7 +236,7 @@
             out_specs=[columns(features // 2)] * 2,
         ),
         out_shape=[jax.ShapeDtypeStruct((features // 2, width), jnp.float32)] * 2,
-        compiler_params=pltpu.CompilerParams(vmem_limit_bytes=56 * 2**20),
+        compiler_params=pltpu.CompilerParams(vmem_limit_bytes=28 * 2**20),
     )(jnp.stack([core, *order]).astype(jnp.int32), pair, from_right, *far, from_left, back_all)
 
 
@@ -247,12 +266,12 @@
     return lax.ppermute(values, axis, [(i, (i + by) % size) for i in range(size)])
 
 
-def to_feature_owner(values, lows, depth, cores, ring, highs):
+def to_feature_owner(values, turned, lows, depth, cores, ring, highs):
     place = lambda y_lo, z, core, x, y_hi: (((y_lo * depth + z) * cores + core) * ring + x) * highs + y_hi
     pairs = []
     for y_lo, z, core, x, y_hi in itertools.product(range(lows), range(depth), range(cores), range(ring), range(highs)):
         owner = x * highs + y_hi
-        target = (owner // depth, owner % depth, core, (z + x) % ring, y_lo ^ y_hi ^ (x // 2))
+        target = (owner // depth, owner % depth, core, (z + x) % ring, y_lo ^ y_hi ^ (x // 2) ^ turned)
         pairs.append((place(y_lo, z, core, x, y_hi), place(*target)))
     return lax.ppermute(values, DP + TENSOR, pairs)
 
@@ -277,7 +296,7 @@
     back_mine = take_rows(relayed[:, features:], flat_slots)
 
     inputs_mine = take_rows_across(relayed[:, :features], flat_slots)
-    inputs_mine = to_feature_owner(inputs_mine, lows, depth, cores, ring, highs)
+    pair = jnp.stack([to_feature_owner(inputs_mine, turned, lows, depth, cores, ring, highs) for turned in range(highs)])
 
     projections = (query_proj, key_proj, value_proj)
     block_at = lambda offsets, y: jnp.stack([(x + s) % ring * highs + y for s in offsets]).astype(jnp.int32)
@@ -285,11 +304,8 @@
     part_of = functools.partial(partials, rows=back_mine, projections=projections, features=features)
     near = part_of(block_at(away + (0,), 1 - y_hi), (len(away), 1))
     other_back = shifted(back_mine, "y_lo", 1)
-    inputs_mine, other_back, near = lax.optimization_barrier((inputs_mine, other_back, near))
     copies = jnp.broadcast_to(jnp.stack([back_mine, other_back])[None], (depth, lows) + back_mine.shape)
-    inputs_near = shifted(inputs_mine, "y_hi", 1)
-    inputs_near, copies, near = lax.optimization_barrier((inputs_near, copies, near))
-    pair = jnp.stack([inputs_mine, inputs_near])
+    pair, copies, near = lax.optimization_barrier((pair, copies, near))
     near_away, near_here = [shifted(block, "y_hi", 1) for block in near]
     back_all = lax.all_to_all(copies, "z", split_axis=0, concat_axis=0, tiled=True).reshape(-1, width)
     source_x = y_lo * (depth // highs) + z // highs
@@ -298,9 +314,8 @@
 
     from_left, from_right = shifted(pair, "x", 1), shifted(pair, "x", -1)
     places = jnp.stack([(x + s) % ring for s in away]).astype(jnp.int32)
-    (to_others,) = part_of(
-        block_at(away, y_hi), (len(away),), arrived=((near_away, jnp.arange(len(away))),), places=places
-    )
+    (own_away,) = part_of(block_at(away, y_hi), (len(away),), coded_out=False)
+    to_others = recoded(own_away, near_away, places)
     far = [shifted(from_left[:1], "x", 1), shifted(from_right[1:], "x", -1)]
     from_others = lax.all_to_all(to_others, "x", split_axis=0, concat_axis=0, tiled=True)
     far, near_here, _ = lax.optimization_barrier((far, near_here, to_others))
@@ -308,7 +323,8 @@
     for_other, weight_grad = weight_halves(core, order, pair, from_right, far, from_left, back_all, 2 * key_width)
     from_other = shifted(for_other, "core", 1)
     grads = summed_columns(weight_grad, from_other, (query_width, key_width, key_width))
-    (here,) = part_of(block_at((0,), y_hi), (1,), arrived=((near_here, jnp.zeros(1)),), coded_out=False)
+    (here,) = part_of(block_at((0,), y_hi), (1,), arrived=(near_here,), coded_out=False)
+    here, *grads = lax.optimization_barrier((here, *grads))
     return *grads, decoded_sum(here[0], from_others, places)
 
 

time: 167 us -> 161 us (0.964); the launches traced: 164 us -> 160 us
  waiting for transfers between devices: 80.2 us -> 67.3 us
  starting transfers between devices: 27.1 us -> 30.8 us
  Pallas kernels: 38.4 us -> 41.3 us
  local copies, waits for them, and re-layouts: 10.4 us -> 12.9 us
    ppermute x9 -> x8, waiting for transfers between devices: 41.3 us -> 20.5 us  [shifted(): lax.ppermute(values, axis, [(i, (i + by) % size) for i in range(size)])]
    ppermute x1 -> x2, waiting for transfers between devices: 7.84 us -> 19.1 us  [to_feature_owner(): return lax.ppermute(values, DP + TENSOR, pairs)]
    pallas_call x0 -> x1, Pallas kernels: none -> 5.58 us  [recoded(): pl.pallas_call(recode_kernel, grid_spec=pltpu.PrefetchScalarGridSpec(num_...]
    unnamed x14 -> x16, local copies, waits for them, and re-layouts: 4.15 us -> 7.92 us
    all_to_all x1, waiting for transfers between devices: 8.56 us -> 5.19 us  [body(): lax.all_to_all(to_others, 'x', split_axis=0, concat_axis=0, tiled=True)]
    pallas_call x1, Pallas kernels: 8.42 us -> 6.59 us  [weight_halves(): pl.pallas_call(weight_kernel, grid_spec=pltpu.PrefetchScalarGridSpec(num_...]
    ppermute x9 -> x8, starting transfers between devices: 10.2 us -> 11.8 us  [shifted(): lax.ppermute(values, axis, [(i, (i + by) % size) for i in range(size)])]
    ppermute x1 -> x2, starting transfers between devices: 2.65 us -> 4.05 us  [to_feature_owner(): return lax.ppermute(values, DP + TENSOR, pairs)]
  transfers between devices with their start and end apart: 13 -> 13, of which waited for: 7 -> 6; matrix products, arithmetic and copies ran while one was open for 6% -> 4% of each run, Pallas kernels for 18% -> 21%
where the time goes in v1:
time: 161 us; the launch traced here: 160 us
  waiting for transfers between devices  67.3 us (42%)
  Pallas kernels  41.3 us (26%)
  starting transfers between devices  30.8 us (19%)
  local copies, waits for them, and re-layouts  12.9 us (8%)
  other arithmetic  5.43 us (3%)
    all_to_all x1, waiting for transfers between devices, body(): lax.all_to_all(packed, DP, split_axis=0, concat_axis=0, tiled=True)  22.5 us
    ppermute x8, waiting for transfers between devices, shifted(): lax.ppermute(values, axis, [(i, (i + by) % size) for i in range(size)])  20.5 us
    ppermute x2, waiting for transfers between devices, to_feature_owner(): return lax.ppermute(values, DP + TENSOR, pairs)  19.1 us
    pallas_call x3, Pallas kernels, partials(): pl.pallas_call(functools.partial(partial_kernel, sizes, len(arrived), cod...  17.4 us
    ppermute x8, starting transfers between devices, shifted(): lax.ppermute(values, axis, [(i, (i + by) % size) for i in range(size)])  11.8 us
    unnamed x16, local copies, waits for them, and re-layouts  7.92 us
    all_to_all x1, starting transfers between devices, body(): lax.all_to_all(packed, DP, split_axis=0, concat_axis=0, tiled=True)  6.79 us
    pallas_call x1, Pallas kernels, weight_halves(): pl.pallas_call(weight_kernel, grid_spec=pltpu.PrefetchScalarGridSpec(num_...  6.59 us
  transfers between devices with their start and end apart: 13, of which 6 were waited for; matrix products, arithmetic and copies ran while one was open for 4% of the time, Pallas kernels for 21%

profile of v1, /device:TPU:24, one launch (start us, length us, event | category | flops | bytes accessed | tf_op | source)
XLA Modules:
  0.0 159.6 jit_solution(11207269828566881481)
XLA Ops:
  2.0 4.4 %shard_map.111 = bf16[512,1792]{1,0:T(8,128)(2,1)} custom-call(s32[1]{0:T(128)} %bitcast.1.me_ref, s32[16,256]{1,0:T(8,128)} %reshape.28.slots_ref, bf16[512,1024]{1,0:T(8,128)(2,1)} %refs_0_.1, bf16[512,512]{1,0:T(8,128)(2,1)} %refs_1_.1, bf16[512,128]{1,0:T(8,128)(2,1)} %refs_2_.1, bf16[512,128]{1,0:T(8,128)(2,1)} %refs_3_.1), custom_call_target="tpu_custom_call" | custom-call | tf_op jit(solution)/shard_map/pallas_call | solution.py:61
  6.3 6.8 %all-to-all-start = ((bf16[16,32,1792]{2,1,0:T(8,128)(2,1)}), bf16[16,32,1792]{2,1,0:T(8,128)(2,1)S(1)}, u32[]{:S(2)}, u32[]{:S(2)}) async-start(bf16[16,32,1792]{2,1,0:T(8,128)(2,1)} %bitcast.30), calls=%async_computation | async-start | bytes 3670016 | tf_op jit(solution)/shard_map/all_to_all | solution.py:295
  14.7 22.5 %all-to-all-done = bf16[16,32,1792]{2,1,0:T(8,128)(2,1)S(1)} async-done(((bf16[16,32,1792]{2,1,0:T(8,128)(2,1)}), bf16[16,32,1792]{2,1,0:T(8,128)(2,1)S(1)}, u32[]{:S(2)}, u32[]{:S(2)}) %all-to-all-start) | async-done | bytes 1835040 | tf_op jit(solution)/shard_map/all_to_all | solution.py:295
  37.6 1.7 %collective-permute-start.2 = (bf16[256,768]{1,0:T(8,128)(2,1)S(1)}, bf16[256,768]{1,0:T(8,128)(2,1)S(1)}, u32[]{:S(2)}, u32[]{:S(2)}) collective-permute-start(bf16[256,768]{1,0:T(8,128)(2,1)S(1)} %convolution_convert_fusion.1.rows_ref), channel_id=1, source_target_pairs={{0,64},{64,0},{1,65},{65,1},{2,66},{66,2},{3,67},{67,3},{4,68},{68... | collective-permute-start | bytes 1179656 | tf_op jit(solution)/shard_map/ppermute | solution.py:266
  39.9 2.3 %collective-permute-start = (bf16[1024,256]{1,0:T(8,128)(2,1)S(1)}, bf16[1024,256]{1,0:T(8,128)(2,1)S(1)}, u32[]{:S(2)}, u32[]{:S(2)}) collective-permute-start(bf16[1024,256]{1,0:T(8,128)(2,1)S(1)} %convolution_convert_fusion), channel_id=1, source_target_pairs={{0,0},{1,17},{2,34},{3,51},{4,69},{5,84},{6,103},{7,118},{8,8},{9,... | collective-permute-start | bytes 1572872 | tf_op jit(solution)/shard_map/ppermute | solution.py:276
  42.2 1.8 %collective-permute-start.1 = (bf16[1024,256]{1,0:T(8,128)(2,1)S(1)}, bf16[1024,256]{1,0:T(8,128)(2,1)S(1)}, u32[]{:S(2)}, u32[]{:S(2)}) collective-permute-start(bf16[1024,256]{1,0:T(8,128)(2,1)S(1)} %convolution_convert_fusion), channel_id=1, source_target_pairs={{0,1},{1,16},{2,35},{3,50},{4,68},{5,85},{6,102},{7,119},{8,9},{9,... | collective-permute-start | bytes 1572872 | tf_op jit(solution)/shard_map/ppermute | solution.py:276
  44.5 7.5 %shard_map.112 = (s16[3,272,1024]{2,1,0:T(8,128)(2,1)}, s16[1,272,1024]{2,1,0:T(8,128)(2,1)}) custom-call(s32[4]{0:T(128)} %pad_add_fusion.order_ref, bf16[256,768]{1,0:T(8,128)(2,1)} %copy-done.6, bf16[8192,512]{1,0:T(8,128)(2,1)} %query_ref.5, bf16[8192,128]{1,0:T(8,128)(2,1)} %key_ref.5, bf16[8192,128]{1,0:T(8,128)(2,1)} %value_ref.5), custom_call_target="tpu_custom_call" | custom-call | tf_op jit(solution)/shard_map/pallas_call | solution.py:142
  53.1 11.0 %collective-permute-done = bf16[1024,256]{1,0:T(8,128)(2,1)S(1)} collective-permute-done((bf16[1024,256]{1,0:T(8,128)(2,1)S(1)}, bf16[1024,256]{1,0:T(8,128)(2,1)S(1)}, u32[]{:S(2)}, u32[]{:S(2)}) %collective-permute-start) | collective-permute-done | bytes 524320 | tf_op jit(solution)/shard_map/ppermute | solution.py:276
  64.1 8.1 %collective-permute-done.1 = bf16[1024,256]{1,0:T(8,128)(2,1)S(1)} collective-permute-done((bf16[1024,256]{1,0:T(8,128)(2,1)S(1)}, bf16[1024,256]{1,0:T(8,128)(2,1)S(1)}, u32[]{:S(2)}, u32[]{:S(2)}) %collective-permute-start.1) | collective-permute-done | bytes 524320 | tf_op jit(solution)/shard_map/ppermute | solution.py:276
  73.3 1.8 %broadcast_in_dim.2 = bf16[4,2,256,768]{3,2,1,0:T(8,128)(2,1)} broadcast(bf16[2,256,768]{2,1,0:T(8,128)(2,1)S(1)} %pad_maximum_fusion.1), dimensions={1,2,3} | broadcast | bytes 3932160 | tf_op jit(solution)/shard_map/broadcast_in_dim | solution.py:307
  75.2 3.7 %all-to-all-start.1 = ((bf16[4,2,256,768]{3,2,1,0:T(8,128)(2,1)}), bf16[4,2,256,768]{3,2,1,0:T(8,128)(2,1)S(1)}, u32[]{:S(2)}, u32[]{:S(2)}) async-start(bf16[4,2,256,768]{3,2,1,0:T(8,128)(2,1)} %broadcast_in_dim.2), calls=%async_computation.1 | async-start | bytes 6291456 | tf_op jit(solution)/shard_map/all_to_all | solution.py:310
  78.9 1.9 %collective-permute-start.8 = (s16[3,272,1024]{2,1,0:T(8,128)(2,1)}, s16[3,272,1024]{2,1,0:T(8,128)(2,1)}, u32[]{:S(2)}, u32[]{:S(2)}) collective-permute-start(s16[3,272,1024]{2,1,0:T(8,128)(2,1)} %get-tuple-element.26), channel_id=1, source_target_pairs={{0,1},{1,0},{2,3},{3,2},{4,5},{5,4},{6,7},{7,6},{8,9},{9,8},{10,11... | collective-permute-start | bytes 5013512 | tf_op jit(solution)/shard_map/ppermute | solution.py:266
  81.1 3.0 %collective-permute-start.5 = (bf16[2,1024,256]{2,1,0:T(8,128)(2,1)}, bf16[2,1024,256]{2,1,0:T(8,128)(2,1)S(1)}, u32[]{:S(2)}, u32[]{:S(2)}) collective-permute-start(bf16[2,1024,256]{2,1,0:T(8,128)(2,1)} %pad_maximum_fusion.pair_ref), channel_id=1, source_target_pairs={{0,6},{2,0},{4,2},{6,4},{1,7},{3,1},{5,3},{7,5},{8,14},{10,8},{12,... | collective-permute-start | bytes 3145736 | tf_op jit(solution)/shard_map/ppermute | solution.py:266
  84.0 1.7 %collective-permute-start.7 = (s16[1,272,1024]{2,1,0:T(8,128)(2,1)}, s16[1,272,1024]{2,1,0:T(8,128)(2,1)}, u32[]{:S(2)}, u32[]{:S(2)}) collective-permute-start(s16[1,272,1024]{2,1,0:T(8,128)(2,1)} %get-tuple-element.25), channel_id=1, source_target_pairs={{0,1},{1,0},{2,3},{3,2},{4,5},{5,4},{6,7},{7,6},{8,9},{9,8},{10,11... | collective-permute-start | bytes 1671176 | tf_op jit(solution)/shard_map/ppermute | solution.py:266
  85.7 20.2 %collective-permute-done.3.left_ref = bf16[2,1024,256]{2,1,0:T(8,128)(2,1)S(1)} collective-permute-done((bf16[2,1024,256]{2,1,0:T(8,128)(2,1)}, bf16[2,1024,256]{2,1,0:T(8,128)(2,1)S(1)}, u32[]{:S(2)}, u32[]{:S(2)}) %collective-permute-start.3) | collective-permute-done | bytes 1048608 | tf_op jit(solution)/shard_map/ppermute | solution.py:266
  109.5 3.2 %collective-permute-start.6 = (bf16[1,1024,256]{2,1,0:T(8,128)(2,1)}, bf16[1,1024,256]{2,1,0:T(8,128)(2,1)}, u32[]{:S(2)}, u32[]{:S(2)}) collective-permute-start(bf16[1,1024,256]{2,1,0:T(8,128)(2,1)} %slice.23), channel_id=1, source_target_pairs={{0,6},{2,0},{4,2},{6,4},{1,7},{3,1},{5,3},{7,5},{8,14},{10,8},{12,... | collective-permute-start | bytes 1572872 | tf_op jit(solution)/shard_map/ppermute | solution.py:266
  113.9 6.6 %shard_map.113.own_ref = f32[3,256,1024]{2,1,0:T(8,128)} custom-call(s32[3]{0:T(128)} %pad_add_fusion.2.order_ref, bf16[256,768]{1,0:T(8,128)(2,1)} %copy-done.6, bf16[8192,512]{1,0:T(8,128)(2,1)} %query_ref.5, bf16[8192,128]{1,0:T(8,128)(2,1)} %key_ref.5, bf16[8192,128]{1,0:T(8,128)(2,1)} %value_ref.5), custom_call_target="tpu_custom_call" | custom-call | tf_op jit(solution)/shard_map/pallas_call | solution.py:142
  120.5 5.6 %shard_map.114 = s16[4,272,1024]{2,1,0:T(8,128)(2,1)} custom-call(s32[3]{0:T(128)} %pad_add_fusion.1.places_ref.plan_ref, f32[3,256,1024]{2,1,0:T(8,128)} %shard_map.113.own_ref, s16[3,272,1024]{2,1,0:T(8,128)(2,1)} %collective-permute-done.8.near_ref), custom_call_target="tpu_custom_call" | custom-call | tf_op jit(solution)/shard_map/pallas_call | solution.py:166
  126.0 4.5 %all-to-all-start.2 = ((s16[4,272,1024]{2,1,0:T(8,128)(2,1)}), s16[4,272,1024]{2,1,0:T(8,128)(2,1)}, u32[]{:S(2)}, u32[]{:S(2)}) async-start(s16[4,272,1024]{2,1,0:T(8,128)(2,1)} %shard_map.114), calls=%async_computation.2 | async-start | bytes 4456448 | tf_op jit(solution)/shard_map/all_to_all | solution.py:320
  134.4 6.6 %shard_map.116 = (f32[512,768]{1,0:T(8,128)}, f32[512,768]{1,0:T(8,128)S(1)}) custom-call(s32[9]{0:T(128)S(1)} %stack.119.plan_ref, bf16[2,1024,256]{2,1,0:T(8,128)(2,1)S(1)} %copy-done, bf16[2,1024,256]{2,1,0:T(8,128)(2,1)S(1)} %copy-done.4, bf16[1,1024,256]{2,1,0:T(8,128)(2,1)} %collective-permute-done.4.far_0_ref, ...), custom_call_target="tpu_custom_call" | custom-call | tf_op jit(solution)/shard_map/pallas_call | solution.py:230
  142.2 3.3 %shard_map.115 = f32[1,256,1024]{2,1,0:T(8,128)} custom-call(s32[1]{0:T(128)} %bitcast.order_ref, bf16[256,768]{1,0:T(8,128)(2,1)} %copy-done.6, bf16[8192,512]{1,0:T(8,128)(2,1)} %query_ref.5, bf16[8192,128]{1,0:T(8,128)(2,1)} %key_ref.5, bf16[8192,128]{1,0:T(8,128)(2,1)} %value_ref.5, s16[1,272,1024]{2,1,0:T(8,128)(2,1)} %collective-permute-done.7.refs_0_), custom_call_target="tpu_custom_call" | custom-call | tf_op jit(solution)/shard_map/pallas_call | solution.py:142
  147.0 3.8 %shard_map.117 = (f32[512,512]{1,0:T(8,128)}, f32[512,128]{1,0:T(8,128)}, f32[512,128]{1,0:T(8,128)}) custom-call(f32[512,768]{1,0:T(8,128)} %copy-done.5, f32[512,768]{1,0:T(8,128)} %copy-done.7), custom_call_target="tpu_custom_call" | custom-call | tf_op jit(solution)/shard_map/pallas_call | solution.py:255
  150.8 5.2 %all-to-all-done.2.refs_0_.refs_1_.refs_2_.refs_3_.refs_4_.refs_5_ = s16[4,272,1024]{2,1,0:T(8,128)(2,1)} async-done(((s16[4,272,1024]{2,1,0:T(8,128)(2,1)}), s16[4,272,1024]{2,1,0:T(8,128)(2,1)}, u32[]{:S(2)}, u32[]{:S(2)}) %all-to-all-start.2) | async-done | bytes 2228256 | tf_op jit(solution)/shard_map/all_to_all | solution.py:320
  156.0 3.6 %shard_map.118 = f32[256,1024]{1,0:T(8,128)} custom-call(s32[3]{0:T(128)} %pad_add_fusion.1.places_ref.plan_ref, f32[256,1024]{1,0:T(8,128)} %bitcast.32, s16[4,272,1024]{2,1,0:T(8,128)(2,1)} %all-to-all-done.2.refs_0_.refs_1_.refs_2_.refs_3_.refs_4_.refs_5_, s16[4,272,1024]{2,1,0:T(8,128)(2,1)} %all-to-all-done.2.refs_0_.refs_1_.refs_2_.refs_3_.refs_4_.refs_5_, ...), custom_call_target="tpu_custom_call" | custom-call | tf_op jit(solution)/shard_map/pallas_call | solution.py:202
  (41 shorter events, 18.1 us)
Async XLA Ops:
  6.3 30.9 %all-to-all-start = ((bf16[16,32,1792]{2,1,0:T(8,128)(2,1)}), bf16[16,32,1792]{2,1,0:T(8,128)(2,1)S(1)}, u32[]{:S(2)}, u32[]{:S(2)}) async-start(bf16[16,32,1792]{2,1,0:T(8,128)(2,1)} %bitcast.30), calls=%async_computation | async-start | bytes 3670016 | tf_op jit(solution)/shard_map/all_to_all | solution.py:295
  37.6 6.9 %copy-start.6 = (bf16[256,768]{1,0:T(8,128)(2,1)}, bf16[256,768]{1,0:T(8,128)(2,1)S(1)}, u32[]{:S(2)}) copy-start(bf16[256,768]{1,0:T(8,128)(2,1)S(1)} %convolution_convert_fusion.1.rows_ref) | copy-start | bytes 1179652
  37.6 14.4 %collective-permute-start.2 = (bf16[256,768]{1,0:T(8,128)(2,1)S(1)}, bf16[256,768]{1,0:T(8,128)(2,1)S(1)}, u32[]{:S(2)}, u32[]{:S(2)}) collective-permute-start(bf16[256,768]{1,0:T(8,128)(2,1)S(1)} %convolution_convert_fusion.1.rows_ref), channel_id=1, source_target_pairs={{0,64},{64,0},{1,65},{65,1},{2,66},{66,2},{3,67},{67,3},{4,68},{68... | collective-permute-start | bytes 1179656 | tf_op jit(solution)/shard_map/ppermute | solution.py:266
  39.9 24.2 %collective-permute-start = (bf16[1024,256]{1,0:T(8,128)(2,1)S(1)}, bf16[1024,256]{1,0:T(8,128)(2,1)S(1)}, u32[]{:S(2)}, u32[]{:S(2)}) collective-permute-start(bf16[1024,256]{1,0:T(8,128)(2,1)S(1)} %convolution_convert_fusion), channel_id=1, source_target_pairs={{0,0},{1,17},{2,34},{3,51},{4,69},{5,84},{6,103},{7,118},{8,8},{9,... | collective-permute-start | bytes 1572872 | tf_op jit(solution)/shard_map/ppermute | solution.py:276
  42.2 30.1 %collective-permute-start.1 = (bf16[1024,256]{1,0:T(8,128)(2,1)S(1)}, bf16[1024,256]{1,0:T(8,128)(2,1)S(1)}, u32[]{:S(2)}, u32[]{:S(2)}) collective-permute-start(bf16[1024,256]{1,0:T(8,128)(2,1)S(1)} %convolution_convert_fusion), channel_id=1, source_target_pairs={{0,1},{1,16},{2,35},{3,50},{4,68},{5,85},{6,102},{7,119},{8,9},{9,... | collective-permute-start | bytes 1572872 | tf_op jit(solution)/shard_map/ppermute | solution.py:276
  75.2 50.9 %all-to-all-start.1 = ((bf16[4,2,256,768]{3,2,1,0:T(8,128)(2,1)}), bf16[4,2,256,768]{3,2,1,0:T(8,128)(2,1)S(1)}, u32[]{:S(2)}, u32[]{:S(2)}) async-start(bf16[4,2,256,768]{3,2,1,0:T(8,128)(2,1)} %broadcast_in_dim.2), calls=%async_computation.1 | async-start | bytes 6291456 | tf_op jit(solution)/shard_map/all_to_all | solution.py:310
  78.9 41.6 %collective-permute-start.8 = (s16[3,272,1024]{2,1,0:T(8,128)(2,1)}, s16[3,272,1024]{2,1,0:T(8,128)(2,1)}, u32[]{:S(2)}, u32[]{:S(2)}) collective-permute-start(s16[3,272,1024]{2,1,0:T(8,128)(2,1)} %get-tuple-element.26), channel_id=1, source_target_pairs={{0,1},{1,0},{2,3},{3,2},{4,5},{5,4},{6,7},{7,6},{8,9},{9,8},{10,11... | collective-permute-start | bytes 5013512 | tf_op jit(solution)/shard_map/ppermute | solution.py:266
  80.8 25.1 %collective-permute-start.3 = (bf16[2,1024,256]{2,1,0:T(8,128)(2,1)}, bf16[2,1024,256]{2,1,0:T(8,128)(2,1)S(1)}, u32[]{:S(2)}, u32[]{:S(2)}) collective-permute-start(bf16[2,1024,256]{2,1,0:T(8,128)(2,1)} %pad_maximum_fusion.pair_ref), channel_id=1, source_target_pairs={{0,2},{2,4},{4,6},{6,0},{1,3},{3,5},{5,7},{7,1},{8,10},{10,12},{12... | collective-permute-start | bytes 3145736 | tf_op jit(solution)/shard_map/ppermute | solution.py:266
  81.1 26.6 %collective-permute-start.5 = (bf16[2,1024,256]{2,1,0:T(8,128)(2,1)}, bf16[2,1024,256]{2,1,0:T(8,128)(2,1)S(1)}, u32[]{:S(2)}, u32[]{:S(2)}) collective-permute-start(bf16[2,1024,256]{2,1,0:T(8,128)(2,1)} %pad_maximum_fusion.pair_ref), channel_id=1, source_target_pairs={{0,6},{2,0},{4,2},{6,4},{1,7},{3,1},{5,3},{7,5},{8,14},{10,8},{12,... | collective-permute-start | bytes 3145736 | tf_op jit(solution)/shard_map/ppermute | solution.py:266
  84.0 46.7 %collective-permute-start.7 = (s16[1,272,1024]{2,1,0:T(8,128)(2,1)}, s16[1,272,1024]{2,1,0:T(8,128)(2,1)}, u32[]{:S(2)}, u32[]{:S(2)}) collective-permute-start(s16[1,272,1024]{2,1,0:T(8,128)(2,1)} %get-tuple-element.25), channel_id=1, source_target_pairs={{0,1},{1,0},{2,3},{3,2},{4,5},{5,4},{6,7},{7,6},{8,9},{9,8},{10,11... | collective-permute-start | bytes 1671176 | tf_op jit(solution)/shard_map/ppermute | solution.py:266
  106.7 1.0 copy-start.1
  107.7 23.0 %collective-permute-start.4 = (bf16[1,1024,256]{2,1,0:T(8,128)(2,1)}, bf16[1,1024,256]{2,1,0:T(8,128)(2,1)}, u32[]{:S(2)}, u32[]{:S(2)}) collective-permute-start(bf16[1,1024,256]{2,1,0:T(8,128)(2,1)} %slice.22), channel_id=1, source_target_pairs={{0,2},{2,4},{4,6},{6,0},{1,3},{3,5},{5,7},{7,1},{8,10},{10,12},{12... | collective-permute-start | bytes 1572872 | tf_op jit(solution)/shard_map/ppermute | solution.py:266
  108.5 1.0 copy-start.3
  109.5 21.2 %collective-permute-start.6 = (bf16[1,1024,256]{2,1,0:T(8,128)(2,1)}, bf16[1,1024,256]{2,1,0:T(8,128)(2,1)}, u32[]{:S(2)}, u32[]{:S(2)}) collective-permute-start(bf16[1,1024,256]{2,1,0:T(8,128)(2,1)} %slice.23), channel_id=1, source_target_pairs={{0,6},{2,0},{4,2},{6,4},{1,7},{3,1},{5,3},{7,5},{8,14},{10,8},{12,... | collective-permute-start | bytes 1572872 | tf_op jit(solution)/shard_map/ppermute | solution.py:266
  126.0 30.0 %all-to-all-start.2 = ((s16[4,272,1024]{2,1,0:T(8,128)(2,1)}), s16[4,272,1024]{2,1,0:T(8,128)(2,1)}, u32[]{:S(2)}, u32[]{:S(2)}) async-start(s16[4,272,1024]{2,1,0:T(8,128)(2,1)} %shard_map.114), calls=%async_computation.2 | async-start | bytes 4456448 | tf_op jit(solution)/shard_map/all_to_all | solution.py:320
  130.8 1.2 copy-start
  132.0 1.2 copy-start.2
  133.2 1.2 copy-start.4
  141.0 1.2 copy-start.5
  142.2 3.6 %collective-permute-start.9 = (f32[512,768]{1,0:T(8,128)}, f32[512,768]{1,0:T(8,128)S(1)}, u32[]{:S(2)}, u32[]{:S(2)}) collective-permute-start(f32[512,768]{1,0:T(8,128)} %get-tuple-element.32), channel_id=1, source_target_pairs={{0,8},{8,0},{1,9},{9,1},{2,10},{10,2},{3,11},{11,3},{4,12},{12,4},... | collective-permute-start | bytes 4718600 | tf_op jit(solution)/shard_map/ppermute | solution.py:266
  145.8 1.1 copy-start.7

commit v2 on v1

--- a/solution.py
+++ b/solution.py
@@ -13,7 +13,8 @@
 DP = tuple(name for name, _ in DP_SIZES)
 TENSOR = tuple(name for name, _ in TENSOR_SIZES)
 SCALE_ROWS = 16
-FRACTION_BITS = 15
+LARGEST = 32766.0
+TO_WHOLE = 1.5 * 2.0**23
 
 
 def balanced_slots(source, dp_count, per_pair):
@@ -87,7 +88,8 @@
 
 
 def decoded(coded, exponent, tokens):
-    step = jnp.exp2(column_of(exponent.astype(jnp.int32).astype(jnp.float32)[:1], tokens) - FRACTION_BITS)
+    exponent = exponent.astype(jnp.int32).astype(jnp.float32)[:1]
+    step = jnp.exp2(column_of(exponent, tokens)) * (1.0 / LARGEST)
     return coded.astype(jnp.int32).astype(jnp.float32) * step
 
 
@@ -95,8 +97,8 @@
     tokens, width = part.shape
     most = jnp.max(jnp.abs(part), axis=1, keepdims=True)
     exponent = jnp.floor(jnp.log2(jnp.maximum(most, 2.0**-100))) + 1.0
-    coded = jnp.round(part * jnp.exp2(FRACTION_BITS - exponent))
-    coded = jnp.clip(coded, -32767.0, 32767.0).astype(jnp.int32).astype(jnp.int16)
+    scaled = part * (jnp.exp2(-exponent) * LARGEST)
+    coded = ((scaled + TO_WHOLE) - TO_WHOLE).astype(jnp.int32).astype(jnp.int16)
     across = jnp.transpose(jnp.broadcast_to(exponent, (tokens, 128)))[:SCALE_ROWS, :]
     across = jnp.concatenate([across, jnp.zeros((SCALE_ROWS, width - tokens), jnp.float32)], axis=1)
     return coded, across.astype(jnp.int32).astype(jnp.int16)
@@ -190,7 +192,7 @@
 
 def decoded_sum(here, arrived, places):
     tokens, features = here.shape
-    step = features // 2
+    step = features
     columns = pl.BlockSpec((tokens, step), lambda j, plan_ref: (0, j))
     in_specs, operands = [columns], [here]
     for i in range(places.shape[0]):
@@ -302,9 +304,10 @@
     block_at = lambda offsets, y: jnp.stack([(x + s) % ring * highs + y for s in offsets]).astype(jnp.int32)
     away = (2, 1, ring - 1)
     part_of = functools.partial(partials, rows=back_mine, projections=projections, features=features)
-    near = part_of(block_at(away + (0,), 1 - y_hi), (len(away), 1))
     other_back = shifted(back_mine, "y_lo", 1)
     copies = jnp.broadcast_to(jnp.stack([back_mine, other_back])[None], (depth, lows) + back_mine.shape)
+    rows_after, copies = lax.optimization_barrier((back_mine, copies))
+    near = part_of(block_at(away + (0,), 1 - y_hi), (len(away), 1), rows=rows_after)
     pair, copies, near = lax.optimization_barrier((pair, copies, near))
     near_away, near_here = [shifted(block, "y_hi", 1) for block in near]
     back_all = lax.all_to_all(copies, "z", split_axis=0, concat_axis=0, tiled=True).reshape(-1, width)
@@ -315,6 +318,7 @@
     from_left, from_right = shifted(pair, "x", 1), shifted(pair, "x", -1)
     places = jnp.stack([(x + s) % ring for s in away]).astype(jnp.int32)
     (own_away,) = part_of(block_at(away, y_hi), (len(away),), coded_out=False)
+    from_left, from_right, own_away = lax.optimization_barrier((from_left, from_right, own_away))
     to_others = recoded(own_away, near_away, places)
     far = [shifted(from_left[:1], "x", 1), shifted(from_right[1:], "x", -1)]
     from_others = lax.all_to_all(to_others, "x", split_axis=0, concat_axis=0, tiled=True)

time: 161 us -> 159 us (0.988)
  waiting for transfers between devices: 67.3 us -> 64.1 us
  starting transfers between devices: 30.8 us -> 33.9 us
  local copies, waits for them, and re-layouts: 12.9 us -> 10.6 us
    ppermute x2, waiting for transfers between devices: 19.1 us -> 11.4 us  [to_feature_owner(): return lax.ppermute(values, DP + TENSOR, pairs)]
    unnamed x16 -> x8, local copies, waits for them, and re-layouts: 7.92 us -> 3.53 us
    ppermute x2, starting transfers between devices: 4.05 us -> 6.84 us  [to_feature_owner(): return lax.ppermute(values, DP + TENSOR, pairs)]
    ppermute x8, waiting for transfers between devices: 20.5 us -> 22.8 us  [shifted(): lax.ppermute(values, axis, [(i, (i + by) % size) for i in range(size)])]
    all_to_all x1, waiting for transfers between devices: 5.19 us -> 7.42 us  [body(): lax.all_to_all(to_others, 'x', split_axis=0, concat_axis=0, tiled=True)]
    slice x2, local copies, waits for them, and re-layouts: 1.68 us -> 3.75 us  [body(): far = [shifted(from_left[:1], 'x', 1), shifted(from_right[1:], 'x', -1)]]
  transfers between devices with their start and end apart: 13 -> 13, of which waited for: 6 -> 9; matrix products, arithmetic and copies ran while one was open for 4% -> 6% of each run, Pallas kernels for 21% -> 22%
where the time goes in v2:
time: 159 us; the launch traced here: 158 us
  waiting for transfers between devices  64.1 us (40%)
  Pallas kernels  42.8 us (27%)
  starting transfers between devices  33.9 us (21%)
  local copies, waits for them, and re-layouts  10.6 us (7%)
  other arithmetic  4.56 us (3%)
    ppermute x8, waiting for transfers between devices, shifted(): lax.ppermute(values, axis, [(i, (i + by) % size) for i in range(size)])  22.8 us
    all_to_all x1, waiting for transfers between devices, body(): lax.all_to_all(packed, DP, split_axis=0, concat_axis=0, tiled=True)  22.5 us
    pallas_call x3, Pallas kernels, partials(): pl.pallas_call(functools.partial(partial_kernel, sizes, len(arrived), cod...  17.6 us
    ppermute x2, waiting for transfers between devices, to_feature_owner(): return lax.ppermute(values, DP + TENSOR, pairs)  11.4 us
    ppermute x8, starting transfers between devices, shifted(): lax.ppermute(values, axis, [(i, (i + by) % size) for i in range(size)])  11.2 us
    all_to_all x1, waiting for transfers between devices, body(): lax.all_to_all(to_others, 'x', split_axis=0, concat_axis=0, tiled=True)  7.42 us
    pallas_call x1, Pallas kernels, weight_halves(): pl.pallas_call(weight_kernel, grid_spec=pltpu.PrefetchScalarGridSpec(num_...  7.25 us
    ppermute x2, starting transfers between devices, to_feature_owner(): return lax.ppermute(values, DP + TENSOR, pairs)  6.84 us
  transfers between devices with their start and end apart: 13, of which 9 were waited for; matrix products, arithmetic and copies ran while one was open for 6% of the time, Pallas kernels for 22%

profile of v2, /device:TPU:24, one launch (start us, length us, event | category | flops | bytes accessed | tf_op | source)
XLA Modules:
  0.0 157.6 jit_solution(8731497838064339711)
XLA Ops:
  2.0 4.3 %shard_map.111 = bf16[512,1792]{1,0:T(8,128)(2,1)} custom-call(s32[1]{0:T(128)} %bitcast.1.me_ref, s32[16,256]{1,0:T(8,128)} %reshape.28.slots_ref, bf16[512,1024]{1,0:T(8,128)(2,1)} %refs_0_.1, bf16[512,512]{1,0:T(8,128)(2,1)} %refs_1_.1, bf16[512,128]{1,0:T(8,128)(2,1)} %refs_2_.1, bf16[512,128]{1,0:T(8,128)(2,1)} %refs_3_.1), custom_call_target="tpu_custom_call" | custom-call | tf_op jit(solution)/shard_map/pallas_call | solution.py:62
  6.3 6.8 %all-to-all-start = ((bf16[16,32,1792]{2,1,0:T(8,128)(2,1)}), bf16[16,32,1792]{2,1,0:T(8,128)(2,1)S(1)}, u32[]{:S(2)}, u32[]{:S(2)}) async-start(bf16[16,32,1792]{2,1,0:T(8,128)(2,1)} %bitcast.30), calls=%async_computation | async-start | bytes 3670016 | tf_op jit(solution)/shard_map/all_to_all | solution.py:297
  14.7 22.5 %all-to-all-done = bf16[16,32,1792]{2,1,0:T(8,128)(2,1)S(1)} async-done(((bf16[16,32,1792]{2,1,0:T(8,128)(2,1)}), bf16[16,32,1792]{2,1,0:T(8,128)(2,1)S(1)}, u32[]{:S(2)}, u32[]{:S(2)}) %all-to-all-start) | async-done | bytes 1835040 | tf_op jit(solution)/shard_map/all_to_all | solution.py:297
  40.5 6.2 %collective-permute-start = (bf16[1024,256]{1,0:T(8,128)(2,1)S(1)}, bf16[1024,256]{1,0:T(8,128)(2,1)S(1)}, u32[]{:S(2)}, u32[]{:S(2)}) collective-permute-start(bf16[1024,256]{1,0:T(8,128)(2,1)S(1)} %convolution_convert_fusion), channel_id=1, source_target_pairs={{0,0},{1,17},{2,34},{3,51},{4,69},{5,84},{6,103},{7,118},{8,8},{9,... | collective-permute-start | bytes 1572872 | tf_op jit(solution)/shard_map/ppermute | solution.py:278
  47.5 2.2 %collective-permute-done.2 = bf16[256,768]{1,0:T(8,128)(2,1)S(1)} collective-permute-done((bf16[256,768]{1,0:T(8,128)(2,1)S(1)}, bf16[256,768]{1,0:T(8,128)(2,1)S(1)}, u32[]{:S(2)}, u32[]{:S(2)}) %collective-permute-start.2) | collective-permute-done | bytes 393248 | tf_op jit(solution)/shard_map/ppermute | solution.py:268
  51.7 7.7 %shard_map.112 = (s16[3,272,1024]{2,1,0:T(8,128)(2,1)}, s16[1,272,1024]{2,1,0:T(8,128)(2,1)}) custom-call(s32[4]{0:T(128)} %pad_add_fusion.order_ref, bf16[256,768]{1,0:T(8,128)(2,1)} %copy-done.2, bf16[8192,512]{1,0:T(8,128)(2,1)} %query_ref.5, bf16[8192,128]{1,0:T(8,128)(2,1)} %key_ref.5, bf16[8192,128]{1,0:T(8,128)(2,1)} %value_ref.5), custom_call_target="tpu_custom_call" | custom-call | tf_op jit(solution)/shard_map/pallas_call | solution.py:144
  59.4 3.5 %collective-permute-done.1 = bf16[1024,256]{1,0:T(8,128)(2,1)S(1)} collective-permute-done((bf16[1024,256]{1,0:T(8,128)(2,1)S(1)}, bf16[1024,256]{1,0:T(8,128)(2,1)S(1)}, u32[]{:S(2)}, u32[]{:S(2)}) %collective-permute-start.1) | collective-permute-done | bytes 524320 | tf_op jit(solution)/shard_map/ppermute | solution.py:278
  62.9 7.9 %collective-permute-done = bf16[1024,256]{1,0:T(8,128)(2,1)S(1)} collective-permute-done((bf16[1024,256]{1,0:T(8,128)(2,1)S(1)}, bf16[1024,256]{1,0:T(8,128)(2,1)S(1)}, u32[]{:S(2)}, u32[]{:S(2)}) %collective-permute-start) | collective-permute-done | bytes 524320 | tf_op jit(solution)/shard_map/ppermute | solution.py:278
  71.9 3.9 %all-to-all-start.1 = ((bf16[4,2,256,768]{3,2,1,0:T(8,128)(2,1)}), bf16[4,2,256,768]{3,2,1,0:T(8,128)(2,1)S(1)}, u32[]{:S(2)}, u32[]{:S(2)}) async-start(bf16[4,2,256,768]{3,2,1,0:T(8,128)(2,1)} %broadcast_in_dim.2), calls=%async_computation.1 | async-start | bytes 6291456 | tf_op jit(solution)/shard_map/all_to_all | solution.py:313
  75.8 2.1 %collective-permute-start.8 = (s16[3,272,1024]{2,1,0:T(8,128)(2,1)}, s16[3,272,1024]{2,1,0:T(8,128)(2,1)}, u32[]{:S(2)}, u32[]{:S(2)}) collective-permute-start(s16[3,272,1024]{2,1,0:T(8,128)(2,1)} %get-tuple-element.36), channel_id=1, source_target_pairs={{0,1},{1,0},{2,3},{3,2},{4,5},{5,4},{6,7},{7,6},{8,9},{9,8},{10,11... | collective-permute-start | bytes 5013512 | tf_op jit(solution)/shard_map/ppermute | solution.py:268
  77.9 1.9 %collective-permute-start.4 = (bf16[2,1024,256]{2,1,0:T(8,128)(2,1)}, bf16[2,1024,256]{2,1,0:T(8,128)(2,1)}, u32[]{:S(2)}, u32[]{:S(2)}) collective-permute-start(bf16[2,1024,256]{2,1,0:T(8,128)(2,1)} %pad_maximum_fusion.pair_ref), channel_id=1, source_target_pairs={{0,6},{2,0},{4,2},{6,4},{1,7},{3,1},{5,3},{7,5},{8,14},{10,8},{12,... | collective-permute-start | bytes 3145736 | tf_op jit(solution)/shard_map/ppermute | solution.py:268
  79.9 3.4 %collective-permute-start.7 = (s16[1,272,1024]{2,1,0:T(8,128)(2,1)}, s16[1,272,1024]{2,1,0:T(8,128)(2,1)}, u32[]{:S(2)}, u32[]{:S(2)}) collective-permute-start(s16[1,272,1024]{2,1,0:T(8,128)(2,1)} %get-tuple-element.34), channel_id=1, source_target_pairs={{0,1},{1,0},{2,3},{3,2},{4,5},{5,4},{6,7},{7,6},{8,9},{9,8},{10,11... | collective-permute-start | bytes 1671176 | tf_op jit(solution)/shard_map/ppermute | solution.py:268
  83.8 6.6 %shard_map.113.own_ref = f32[3,256,1024]{2,1,0:T(8,128)} custom-call(s32[3]{0:T(128)} %pad_add_fusion.1.order_ref, bf16[256,768]{1,0:T(8,128)(2,1)} %copy-done.2, bf16[8192,512]{1,0:T(8,128)(2,1)} %query_ref.5, bf16[8192,128]{1,0:T(8,128)(2,1)} %key_ref.5, bf16[8192,128]{1,0:T(8,128)(2,1)} %value_ref.5), custom_call_target="tpu_custom_call" | custom-call | tf_op jit(solution)/shard_map/pallas_call | solution.py:144
  90.4 12.0 %collective-permute-done.4.right_ref = bf16[2,1024,256]{2,1,0:T(8,128)(2,1)} collective-permute-done((bf16[2,1024,256]{2,1,0:T(8,128)(2,1)}, bf16[2,1024,256]{2,1,0:T(8,128)(2,1)}, u32[]{:S(2)}, u32[]{:S(2)}) %collective-permute-start.4) | collective-permute-done | bytes 1048608 | tf_op jit(solution)/shard_map/ppermute | solution.py:268
  102.4 3.4 %collective-permute-done.3.left_ref = bf16[2,1024,256]{2,1,0:T(8,128)(2,1)} collective-permute-done((bf16[2,1024,256]{2,1,0:T(8,128)(2,1)}, bf16[2,1024,256]{2,1,0:T(8,128)(2,1)}, u32[]{:S(2)}, u32[]{:S(2)}) %collective-permute-start.3) | collective-permute-done | bytes 1048608 | tf_op jit(solution)/shard_map/ppermute | solution.py:268
  107.7 1.9 %slice.19 = bf16[1,1024,256]{2,1,0:T(8,128)(2,1)} slice(bf16[2,1024,256]{2,1,0:T(8,128)(2,1)} %collective-permute-done.4.right_ref), slice={[1:2], [0:1024], [0:256]} | slice | bytes 1048576 | tf_op jit(solution)/shard_map/slice | solution.py:323
  112.2 4.9 %collective-permute-done.8.near_ref = s16[3,272,1024]{2,1,0:T(8,128)(2,1)} collective-permute-done((s16[3,272,1024]{2,1,0:T(8,128)(2,1)}, s16[3,272,1024]{2,1,0:T(8,128)(2,1)}, u32[]{:S(2)}, u32[]{:S(2)}) %collective-permute-start.8) | collective-permute-done | bytes 1671200 | tf_op jit(solution)/shard_map/ppermute | solution.py:268
  117.0 5.8 %shard_map.114 = s16[4,272,1024]{2,1,0:T(8,128)(2,1)} custom-call(s32[3]{0:T(128)} %pad_add_fusion.2.places_ref.plan_ref, f32[3,256,1024]{2,1,0:T(8,128)} %shard_map.113.own_ref, s16[3,272,1024]{2,1,0:T(8,128)(2,1)} %collective-permute-done.8.near_ref), custom_call_target="tpu_custom_call" | custom-call | tf_op jit(solution)/shard_map/pallas_call | solution.py:168
  122.8 5.1 %all-to-all-start.2 = ((s16[4,272,1024]{2,1,0:T(8,128)(2,1)}), s16[4,272,1024]{2,1,0:T(8,128)(2,1)}, u32[]{:S(2)}, u32[]{:S(2)}) async-start(s16[4,272,1024]{2,1,0:T(8,128)(2,1)} %shard_map.114), calls=%async_computation.2 | async-start | bytes 4456448 | tf_op jit(solution)/shard_map/all_to_all | solution.py:324
  129.3 7.3 %shard_map.116 = (f32[512,768]{1,0:T(8,128)}, f32[512,768]{1,0:T(8,128)S(1)}) custom-call(s32[9]{0:T(128)S(1)} %stack.119.plan_ref, bf16[2,1024,256]{2,1,0:T(8,128)(2,1)S(1)} %copy-done, bf16[2,1024,256]{2,1,0:T(8,128)(2,1)} %collective-permute-done.4.right_ref, bf16[1,1024,256]{2,1,0:T(8,128)(2,1)} %collective-permute-done.5.far_0_ref, ...), custom_call_target="tpu_custom_call" | custom-call | tf_op jit(solution)/shard_map/pallas_call | solution.py:232
  137.7 3.3 %shard_map.115 = f32[1,256,1024]{2,1,0:T(8,128)} custom-call(s32[1]{0:T(128)} %bitcast.order_ref, bf16[256,768]{1,0:T(8,128)(2,1)} %copy-done.2, bf16[8192,512]{1,0:T(8,128)(2,1)} %query_ref.5, bf16[8192,128]{1,0:T(8,128)(2,1)} %key_ref.5, bf16[8192,128]{1,0:T(8,128)(2,1)} %value_ref.5, s16[1,272,1024]{2,1,0:T(8,128)(2,1)} %collective-permute-done.7.refs_0_), custom_call_target="tpu_custom_call" | custom-call | tf_op jit(solution)/shard_map/pallas_call | solution.py:144
  142.4 3.8 %shard_map.117 = (f32[512,512]{1,0:T(8,128)}, f32[512,128]{1,0:T(8,128)}, f32[512,128]{1,0:T(8,128)}) custom-call(f32[512,768]{1,0:T(8,128)} %copy-done.1, f32[512,768]{1,0:T(8,128)} %copy-done.3), custom_call_target="tpu_custom_call" | custom-call | tf_op jit(solution)/shard_map/pallas_call | solution.py:257
  146.3 7.4 %all-to-all-done.2.refs_0_.refs_1_.refs_2_.refs_3_.refs_4_.refs_5_ = s16[4,272,1024]{2,1,0:T(8,128)(2,1)} async-done(((s16[4,272,1024]{2,1,0:T(8,128)(2,1)}), s16[4,272,1024]{2,1,0:T(8,128)(2,1)}, u32[]{:S(2)}, u32[]{:S(2)}) %all-to-all-start.2) | async-done | bytes 2228256 | tf_op jit(solution)/shard_map/all_to_all | solution.py:324
  153.7 3.9 %shard_map.118 = f32[256,1024]{1,0:T(8,128)} custom-call(s32[3]{0:T(128)} %pad_add_fusion.2.places_ref.plan_ref, f32[256,1024]{1,0:T(8,128)} %bitcast.32, s16[4,272,1024]{2,1,0:T(8,128)(2,1)} %all-to-all-done.2.refs_0_.refs_1_.refs_2_.refs_3_.refs_4_.refs_5_, s16[4,272,1024]{2,1,0:T(8,128)(2,1)} %all-to-all-done.2.refs_0_.refs_1_.refs_2_.refs_3_.refs_4_.refs_5_, ...), custom_call_target="tpu_custom_call" | custom-call | tf_op jit(solution)/shard_map/pallas_call | solution.py:204
  (33 shorter events, 19.0 us)
Async XLA Ops:
  6.3 30.9 %all-to-all-start = ((bf16[16,32,1792]{2,1,0:T(8,128)(2,1)}), bf16[16,32,1792]{2,1,0:T(8,128)(2,1)S(1)}, u32[]{:S(2)}, u32[]{:S(2)}) async-start(bf16[16,32,1792]{2,1,0:T(8,128)(2,1)} %bitcast.30), calls=%async_computation | async-start | bytes 3670016 | tf_op jit(solution)/shard_map/all_to_all | solution.py:297
  37.6 12.2 %copy-start.2 = (bf16[256,768]{1,0:T(8,128)(2,1)}, bf16[256,768]{1,0:T(8,128)(2,1)S(1)}, u32[]{:S(2)}) copy-start(bf16[256,768]{1,0:T(8,128)(2,1)S(1)} %convolution_convert_fusion.1.rows_ref) | copy-start | bytes 1179652
  37.6 12.1 %collective-permute-start.2 = (bf16[256,768]{1,0:T(8,128)(2,1)S(1)}, bf16[256,768]{1,0:T(8,128)(2,1)S(1)}, u32[]{:S(2)}, u32[]{:S(2)}) collective-permute-start(bf16[256,768]{1,0:T(8,128)(2,1)S(1)} %convolution_convert_fusion.1.rows_ref), channel_id=1, source_target_pairs={{0,64},{64,0},{1,65},{65,1},{2,66},{66,2},{3,67},{67,3},{4,68},{68... | collective-permute-start | bytes 1179656 | tf_op jit(solution)/shard_map/ppermute | solution.py:268
  39.9 23.0 %collective-permute-start.1 = (bf16[1024,256]{1,0:T(8,128)(2,1)S(1)}, bf16[1024,256]{1,0:T(8,128)(2,1)S(1)}, u32[]{:S(2)}, u32[]{:S(2)}) collective-permute-start(bf16[1024,256]{1,0:T(8,128)(2,1)S(1)} %convolution_convert_fusion), channel_id=1, source_target_pairs={{0,1},{1,16},{2,35},{3,50},{4,68},{5,85},{6,102},{7,119},{8,9},{9,... | collective-permute-start | bytes 1572872 | tf_op jit(solution)/shard_map/ppermute | solution.py:278
  40.5 30.3 %collective-permute-start = (bf16[1024,256]{1,0:T(8,128)(2,1)S(1)}, bf16[1024,256]{1,0:T(8,128)(2,1)S(1)}, u32[]{:S(2)}, u32[]{:S(2)}) collective-permute-start(bf16[1024,256]{1,0:T(8,128)(2,1)S(1)} %convolution_convert_fusion), channel_id=1, source_target_pairs={{0,0},{1,17},{2,34},{3,51},{4,69},{5,84},{6,103},{7,118},{8,8},{9,... | collective-permute-start | bytes 1572872 | tf_op jit(solution)/shard_map/ppermute | solution.py:278
  71.9 50.9 %all-to-all-start.1 = ((bf16[4,2,256,768]{3,2,1,0:T(8,128)(2,1)}), bf16[4,2,256,768]{3,2,1,0:T(8,128)(2,1)S(1)}, u32[]{:S(2)}, u32[]{:S(2)}) async-start(bf16[4,2,256,768]{3,2,1,0:T(8,128)(2,1)} %broadcast_in_dim.2), calls=%async_computation.1 | async-start | bytes 6291456 | tf_op jit(solution)/shard_map/all_to_all | solution.py:313
  75.8 41.3 %collective-permute-start.8 = (s16[3,272,1024]{2,1,0:T(8,128)(2,1)}, s16[3,272,1024]{2,1,0:T(8,128)(2,1)}, u32[]{:S(2)}, u32[]{:S(2)}) collective-permute-start(s16[3,272,1024]{2,1,0:T(8,128)(2,1)} %get-tuple-element.36), channel_id=1, source_target_pairs={{0,1},{1,0},{2,3},{3,2},{4,5},{5,4},{6,7},{7,6},{8,9},{9,8},{10,11... | collective-permute-start | bytes 5013512 | tf_op jit(solution)/shard_map/ppermute | solution.py:268
  77.9 24.5 %collective-permute-start.4 = (bf16[2,1024,256]{2,1,0:T(8,128)(2,1)}, bf16[2,1024,256]{2,1,0:T(8,128)(2,1)}, u32[]{:S(2)}, u32[]{:S(2)}) collective-permute-start(bf16[2,1024,256]{2,1,0:T(8,128)(2,1)} %pad_maximum_fusion.pair_ref), channel_id=1, source_target_pairs={{0,6},{2,0},{4,2},{6,4},{1,7},{3,1},{5,3},{7,5},{8,14},{10,8},{12,... | collective-permute-start | bytes 3145736 | tf_op jit(solution)/shard_map/ppermute | solution.py:268
  79.8 26.0 %collective-permute-start.3 = (bf16[2,1024,256]{2,1,0:T(8,128)(2,1)}, bf16[2,1024,256]{2,1,0:T(8,128)(2,1)}, u32[]{:S(2)}, u32[]{:S(2)}) collective-permute-start(bf16[2,1024,256]{2,1,0:T(8,128)(2,1)} %pad_maximum_fusion.pair_ref), channel_id=1, source_target_pairs={{0,2},{2,4},{4,6},{6,0},{1,3},{3,5},{5,7},{7,1},{8,10},{10,12},{12... | collective-permute-start | bytes 3145736 | tf_op jit(solution)/shard_map/ppermute | solution.py:268
  79.9 48.1 %collective-permute-start.7 = (s16[1,272,1024]{2,1,0:T(8,128)(2,1)}, s16[1,272,1024]{2,1,0:T(8,128)(2,1)}, u32[]{:S(2)}, u32[]{:S(2)}) collective-permute-start(s16[1,272,1024]{2,1,0:T(8,128)(2,1)} %get-tuple-element.34), channel_id=1, source_target_pairs={{0,1},{1,0},{2,3},{3,2},{4,5},{5,4},{6,7},{7,6},{8,9},{9,8},{10,11... | collective-permute-start | bytes 1671176 | tf_op jit(solution)/shard_map/ppermute | solution.py:268
  109.5 18.5 %collective-permute-start.6 = (bf16[1,1024,256]{2,1,0:T(8,128)(2,1)}, bf16[1,1024,256]{2,1,0:T(8,128)(2,1)}, u32[]{:S(2)}, u32[]{:S(2)}) collective-permute-start(bf16[1,1024,256]{2,1,0:T(8,128)(2,1)} %slice.19), channel_id=1, source_target_pairs={{0,6},{2,0},{4,2},{6,4},{1,7},{3,1},{5,3},{7,5},{8,14},{10,8},{12,... | collective-permute-start | bytes 1572872 | tf_op jit(solution)/shard_map/ppermute | solution.py:268
  109.8 18.2 %collective-permute-start.5 = (bf16[1,1024,256]{2,1,0:T(8,128)(2,1)}, bf16[1,1024,256]{2,1,0:T(8,128)(2,1)}, u32[]{:S(2)}, u32[]{:S(2)}) collective-permute-start(bf16[1,1024,256]{2,1,0:T(8,128)(2,1)} %slice.18), channel_id=1, source_target_pairs={{0,2},{2,4},{4,6},{6,0},{1,3},{3,5},{5,7},{7,1},{8,10},{10,12},{12... | collective-permute-start | bytes 1572872 | tf_op jit(solution)/shard_map/ppermute | solution.py:268
  122.8 30.9 %all-to-all-start.2 = ((s16[4,272,1024]{2,1,0:T(8,128)(2,1)}), s16[4,272,1024]{2,1,0:T(8,128)(2,1)}, u32[]{:S(2)}, u32[]{:S(2)}) async-start(s16[4,272,1024]{2,1,0:T(8,128)(2,1)} %shard_map.114), calls=%async_computation.2 | async-start | bytes 4456448 | tf_op jit(solution)/shard_map/all_to_all | solution.py:324
  128.0 1.2 copy-start
  136.5 1.2 copy-start.1
  137.7 3.6 %collective-permute-start.9 = (f32[512,768]{1,0:T(8,128)}, f32[512,768]{1,0:T(8,128)S(1)}, u32[]{:S(2)}, u32[]{:S(2)}) collective-permute-start(f32[512,768]{1,0:T(8,128)} %get-tuple-element.42), channel_id=1, source_target_pairs={{0,8},{8,0},{1,9},{9,1},{2,10},{10,2},{3,11},{11,3},{4,12},{12,4},... | collective-permute-start | bytes 4718600 | tf_op jit(solution)/shard_map/ppermute | solution.py:268
  141.3 1.1 copy-start.3

commit v3 on v2

--- a/solution.py
+++ b/solution.py
@@ -23,53 +23,66 @@
     return owners * per_pair + jnp.arange(owners.shape[0], dtype=jnp.int32) - owner_start
 
 
-def pack_kernel(per_pair, me_ref, slots_ref, *refs):
-    *value_refs, out_ref = refs
-    slots = slots_ref[...]
-    me = me_ref[0]
-    count, width = slots.shape
-    capacity = value_refs[0].shape[0]
-    first_row = me * capacity
-    lead = slots[:1, :]
-    before = jnp.sum((lead < first_row).astype(jnp.float32)).astype(jnp.int32)
-    mine = jnp.sum(((lead >= first_row) & (lead < first_row + capacity)).astype(jnp.float32)).astype(jnp.int32)
-    moved = pltpu.roll(slots, (width - before) % width, axis=1)
-    lane = lax.broadcasted_iota(jnp.int32, slots.shape, 1)
-    picked = jnp.where(lane < mine, moved - first_row + 1, 0)
-    picked = jnp.concatenate([picked, jnp.zeros((count, capacity - width), jnp.int32)], axis=1)
-    reach = per_pair
-    while reach < capacity:
-        picked = picked + pltpu.roll(picked, reach, axis=1)
-        reach *= 2
-    row = lax.broadcasted_iota(jnp.int32, picked.shape, 0)
-    lane = lax.broadcasted_iota(jnp.int32, picked.shape, 1)
-    own = (lane >= row * per_pair) & (lane < (row + 1) * per_pair)
-    rows = jnp.sum(jnp.where(own, picked, 0).astype(jnp.float32), axis=0, keepdims=True).astype(jnp.int32) - 1
-    chosen = lax.broadcasted_iota(jnp.int32, (capacity, capacity), 0) == rows
-    chosen = jnp.where(chosen, 1.0, 0.0).astype(out_ref.dtype)
-    first = 0
-    for ref in value_refs:
-        taken = lax.dot_general(chosen, ref[...], (((0,), (0,)), ((), ())), preferred_element_type=jnp.float32)
-        out_ref[:, first : first + ref.shape[1]] = taken.astype(out_ref.dtype)
-        first += ref.shape[1]
-
-
-def pack_rows(source, my_index, dp_count, per_pair, values):
-    capacity = values[0].shape[0]
-    width = sum(v.shape[1] for v in values)
-    slots = source.reshape(dp_count, -1)
-    whole = lambda shape: pl.BlockSpec(shape, lambda g, me_ref: (0, 0))
-    return pl.pallas_call(
-        functools.partial(pack_kernel, per_pair),
+def pack_kernel(per_pair, input_steps, me_ref, slots_ref, inputs_ref, query_ref, key_ref, value_ref, out_ref, chosen_ref):
+    capacity = inputs_ref.shape[0]
+    count = capacity // per_pair
+    here, last = pl.program_id(0), pl.num_programs(0) - 1
+
+    @pl.when(here == 0)
+    def _():
+        parts = slots_ref.shape[0] // count
+        slots = jnp.concatenate([slots_ref[pl.ds(i, count, parts), :] for i in range(parts)], axis=1)
+        width = slots.shape[1]
+        first_row = me_ref[0] * capacity
+        lead = slots[:1, :]
+        before = jnp.sum((lead < first_row).astype(jnp.float32)).astype(jnp.int32)
+        mine = jnp.sum(((lead >= first_row) & (lead < first_row + capacity)).astype(jnp.float32)).astype(jnp.int32)
+        moved = pltpu.roll(slots, (width - before) % width, axis=1)
+        lane = lax.broadcasted_iota(jnp.int32, slots.shape, 1)
+        picked = jnp.where(lane < mine, moved - first_row + 1, 0)
+        picked = jnp.concatenate([picked, jnp.zeros((count, capacity - width), jnp.int32)], axis=1)
+        reach = per_pair
+        while reach < capacity:
+            picked = picked + pltpu.roll(picked, reach, axis=1)
+            reach *= 2
+        row = lax.broadcasted_iota(jnp.int32, picked.shape, 0)
+        lane = lax.broadcasted_iota(jnp.int32, picked.shape, 1)
+        own = (lane >= row * per_pair) & (lane < (row + 1) * per_pair)
+        rows = jnp.sum(jnp.where(own, picked, 0).astype(jnp.float32), axis=0, keepdims=True) - 1.0
+        rows = jnp.transpose(jnp.broadcast_to(rows, (128, capacity)))[:, :1].astype(jnp.int32)
+        chosen = lax.broadcasted_iota(jnp.int32, (capacity, capacity), 1) == rows
+        chosen_ref[...] = jnp.where(chosen, 1.0, 0.0).astype(chosen_ref.dtype)
+
+    def take(values):
+        taken = jnp.dot(chosen_ref[...], values, preferred_element_type=jnp.float32)
+        out_ref[...] = taken.astype(out_ref.dtype)
+
+    pl.when(here < input_steps)(lambda: take(inputs_ref[...]))
+    pl.when((here >= input_steps) & (here < last))(lambda: take(query_ref[...]))
+    pl.when(here == last)(lambda: take(jnp.concatenate([key_ref[...], value_ref[...]], axis=1)))
+
+
+def pack_rows(source, my_index, per_pair, inputs, query, key, value):
+    capacity, features = inputs.shape
+    step = 2 * key.shape[1]
+    input_steps, query_steps = features // step, query.shape[1] // step
+    slots = source.reshape(-1, 128)
+    whole = lambda shape: pl.BlockSpec(shape, lambda j, me_ref: (0, 0))
+    chunk = lambda first, n: pl.BlockSpec((capacity, step), lambda j, me_ref: (0, jnp.clip(j - first, 0, n - 1)))
+    steps = input_steps + query_steps + 1
+    return pl.pallas_call(
+        functools.partial(pack_kernel, per_pair, input_steps),
         grid_spec=pltpu.PrefetchScalarGridSpec(
             num_scalar_prefetch=1,
-            grid=(1,),
-            in_specs=[whole(v.shape) for v in (slots, *values)],
-            out_specs=whole((capacity, width)),
-        ),
-        out_shape=jax.ShapeDtypeStruct((capacity, width), values[0].dtype),
+            grid=(steps,),
+            in_specs=[whole(slots.shape), chunk(0, input_steps), chunk(input_steps, query_steps)]
+            + [whole(key.shape), whole(value.shape)],
+            out_specs=pl.BlockSpec((capacity, step), lambda j, me_ref: (0, j)),
+            scratch_shapes=[pltpu.VMEM((capacity, capacity), inputs.dtype)],
+        ),
+        out_shape=jax.ShapeDtypeStruct((capacity, steps * step), inputs.dtype),
         compiler_params=pltpu.CompilerParams(vmem_limit_bytes=62 * 2**20),
-    )(my_index.reshape(1), slots, *values)
+    )(my_index.reshape(1), slots, inputs, query, key, value)
 
 
 def take_rows(values, rows):
@@ -292,7 +305,7 @@
     width = query_width + 2 * key_width
     flat_slots = balanced_slots(source, dp_count, per_pair)
 
-    packed = pack_rows(source, my_index, dp_count, per_pair, (normed, query_back, key_back, value_back))
+    packed = pack_rows(source, my_index, per_pair, normed, query_back, key_back, value_back)
     packed = packed.reshape(dp_count, per_pair, -1)
     relayed = lax.all_to_all(packed, DP, split_axis=0, concat_axis=0, tiled=True).reshape(capacity, -1)
     back_mine = take_rows(relayed[:, features:], flat_slots)

time: 159 us -> 159 us (level)
  Pallas kernels: 42.8 us -> 45 us
    pallas_call x1, Pallas kernels: 4.34 us -> 6.53 us  [pack_rows(): pl.pallas_call(functools.partial(pack_kernel, per_pair, input_steps), gri...]
where the time goes in v3:
time: 159 us; the launch traced here: 158 us
  waiting for transfers between devices  64.1 us (40%)
  Pallas kernels  45 us (28%)
  starting transfers between devices  33.9 us (21%)
  local copies, waits for them, and re-layouts  9.23 us (6%)
  other arithmetic  4.56 us (3%)
    ppermute x8, waiting for transfers between devices, shifted(): lax.ppermute(values, axis, [(i, (i + by) % size) for i in range(size)])  22.8 us
    all_to_all x1, waiting for transfers between devices, body(): lax.all_to_all(packed, DP, split_axis=0, concat_axis=0, tiled=True)  22.5 us
    pallas_call x3, Pallas kernels, partials(): pl.pallas_call(functools.partial(partial_kernel, sizes, len(arrived), cod...  17.7 us
    ppermute x2, waiting for transfers between devices, to_feature_owner(): return lax.ppermute(values, DP + TENSOR, pairs)  11.4 us
    ppermute x8, starting transfers between devices, shifted(): lax.ppermute(values, axis, [(i, (i + by) % size) for i in range(size)])  11.2 us
    all_to_all x1, waiting for transfers between devices, body(): lax.all_to_all(to_others, 'x', split_axis=0, concat_axis=0, tiled=True)  7.42 us
    pallas_call x1, Pallas kernels, weight_halves(): pl.pallas_call(weight_kernel, grid_spec=pltpu.PrefetchScalarGridSpec(num_...  7.25 us
    ppermute x2, starting transfers between devices, to_feature_owner(): return lax.ppermute(values, DP + TENSOR, pairs)  6.83 us
  transfers between devices with their start and end apart: 13, of which 9 were waited for; matrix products, arithmetic and copies ran while one was open for 6% of the time, Pallas kernels for 22%

profile of v3, /device:TPU:24, one launch (start us, length us, event | category | flops | bytes accessed | tf_op | source)
XLA Modules:
  0.0 158.5 jit_solution(16786447568297508382)
XLA Ops:
  0.6 6.5 %shard_map.111 = bf16[512,1792]{1,0:T(8,128)(2,1)} custom-call(s32[1]{0:T(128)} %bitcast.1.me_ref, s32[32,128]{1,0:T(8,128)} %bitcast.39, bf16[512,1024]{1,0:T(8,128)(2,1)} %inputs_ref.1, bf16[512,512]{1,0:T(8,128)(2,1)} %query_ref.4, bf16[512,128]{1,0:T(8,128)(2,1)} %key_ref.4, bf16[512,128]{1,0:T(8,128)(2,1)} %value_ref.4), custom_call_target="tpu_custom_call" | custom-call | tf_op jit(solution)/shard_map/pallas_call | solution.py:73
  7.2 6.8 %all-to-all-start = ((bf16[16,32,1792]{2,1,0:T(8,128)(2,1)}), bf16[16,32,1792]{2,1,0:T(8,128)(2,1)S(1)}, u32[]{:S(2)}, u32[]{:S(2)}) async-start(bf16[16,32,1792]{2,1,0:T(8,128)(2,1)} %bitcast.31), calls=%async_computation | async-start | bytes 3670016 | tf_op jit(solution)/shard_map/all_to_all | solution.py:310
  15.6 22.5 %all-to-all-done = bf16[16,32,1792]{2,1,0:T(8,128)(2,1)S(1)} async-done(((bf16[16,32,1792]{2,1,0:T(8,128)(2,1)}), bf16[16,32,1792]{2,1,0:T(8,128)(2,1)S(1)}, u32[]{:S(2)}, u32[]{:S(2)}) %all-to-all-start) | async-done | bytes 1835040 | tf_op jit(solution)/shard_map/all_to_all | solution.py:310
  41.4 6.2 %collective-permute-start = (bf16[1024,256]{1,0:T(8,128)(2,1)S(1)}, bf16[1024,256]{1,0:T(8,128)(2,1)S(1)}, u32[]{:S(2)}, u32[]{:S(2)}) collective-permute-start(bf16[1024,256]{1,0:T(8,128)(2,1)S(1)} %convolution_convert_fusion), channel_id=1, source_target_pairs={{0,0},{1,17},{2,34},{3,51},{4,69},{5,84},{6,103},{7,118},{8,8},{9,... | collective-permute-start | bytes 1572872 | tf_op jit(solution)/shard_map/ppermute | solution.py:291
  48.3 2.3 %collective-permute-done.2 = bf16[256,768]{1,0:T(8,128)(2,1)S(1)} collective-permute-done((bf16[256,768]{1,0:T(8,128)(2,1)S(1)}, bf16[256,768]{1,0:T(8,128)(2,1)S(1)}, u32[]{:S(2)}, u32[]{:S(2)}) %collective-permute-start.2) | collective-permute-done | bytes 393248 | tf_op jit(solution)/shard_map/ppermute | solution.py:281
  52.5 7.8 %shard_map.112 = (s16[3,272,1024]{2,1,0:T(8,128)(2,1)}, s16[1,272,1024]{2,1,0:T(8,128)(2,1)}) custom-call(s32[4]{0:T(128)} %pad_add_fusion.order_ref, bf16[256,768]{1,0:T(8,128)(2,1)} %copy-done.2, bf16[8192,512]{1,0:T(8,128)(2,1)} %query_ref.7, bf16[8192,128]{1,0:T(8,128)(2,1)} %key_ref.7, bf16[8192,128]{1,0:T(8,128)(2,1)} %value_ref.7), custom_call_target="tpu_custom_call" | custom-call | tf_op jit(solution)/shard_map/pallas_call | solution.py:157
  60.3 3.4 %collective-permute-done.1 = bf16[1024,256]{1,0:T(8,128)(2,1)S(1)} collective-permute-done((bf16[1024,256]{1,0:T(8,128)(2,1)S(1)}, bf16[1024,256]{1,0:T(8,128)(2,1)S(1)}, u32[]{:S(2)}, u32[]{:S(2)}) %collective-permute-start.1) | collective-permute-done | bytes 524320 | tf_op jit(solution)/shard_map/ppermute | solution.py:291
  63.7 7.9 %collective-permute-done = bf16[1024,256]{1,0:T(8,128)(2,1)S(1)} collective-permute-done((bf16[1024,256]{1,0:T(8,128)(2,1)S(1)}, bf16[1024,256]{1,0:T(8,128)(2,1)S(1)}, u32[]{:S(2)}, u32[]{:S(2)}) %collective-permute-start) | collective-permute-done | bytes 524320 | tf_op jit(solution)/shard_map/ppermute | solution.py:291
  72.7 3.9 %all-to-all-start.1 = ((bf16[4,2,256,768]{3,2,1,0:T(8,128)(2,1)}), bf16[4,2,256,768]{3,2,1,0:T(8,128)(2,1)S(1)}, u32[]{:S(2)}, u32[]{:S(2)}) async-start(bf16[4,2,256,768]{3,2,1,0:T(8,128)(2,1)} %broadcast_in_dim.2), calls=%async_computation.1 | async-start | bytes 6291456 | tf_op jit(solution)/shard_map/all_to_all | solution.py:326
  76.7 2.1 %collective-permute-start.8 = (s16[3,272,1024]{2,1,0:T(8,128)(2,1)}, s16[3,272,1024]{2,1,0:T(8,128)(2,1)}, u32[]{:S(2)}, u32[]{:S(2)}) collective-permute-start(s16[3,272,1024]{2,1,0:T(8,128)(2,1)} %get-tuple-element.36), channel_id=1, source_target_pairs={{0,1},{1,0},{2,3},{3,2},{4,5},{5,4},{6,7},{7,6},{8,9},{9,8},{10,11... | collective-permute-start | bytes 5013512 | tf_op jit(solution)/shard_map/ppermute | solution.py:281
  78.7 1.9 %collective-permute-start.4 = (bf16[2,1024,256]{2,1,0:T(8,128)(2,1)}, bf16[2,1024,256]{2,1,0:T(8,128)(2,1)}, u32[]{:S(2)}, u32[]{:S(2)}) collective-permute-start(bf16[2,1024,256]{2,1,0:T(8,128)(2,1)} %pad_maximum_fusion.pair_ref), channel_id=1, source_target_pairs={{0,6},{2,0},{4,2},{6,4},{1,7},{3,1},{5,3},{7,5},{8,14},{10,8},{12,... | collective-permute-start | bytes 3145736 | tf_op jit(solution)/shard_map/ppermute | solution.py:281
  80.8 3.4 %collective-permute-start.7 = (s16[1,272,1024]{2,1,0:T(8,128)(2,1)}, s16[1,272,1024]{2,1,0:T(8,128)(2,1)}, u32[]{:S(2)}, u32[]{:S(2)}) collective-permute-start(s16[1,272,1024]{2,1,0:T(8,128)(2,1)} %get-tuple-element.34), channel_id=1, source_target_pairs={{0,1},{1,0},{2,3},{3,2},{4,5},{5,4},{6,7},{7,6},{8,9},{9,8},{10,11... | collective-permute-start | bytes 1671176 | tf_op jit(solution)/shard_map/ppermute | solution.py:281
  84.7 6.6 %shard_map.113.own_ref = f32[3,256,1024]{2,1,0:T(8,128)} custom-call(s32[3]{0:T(128)} %pad_add_fusion.1.order_ref, bf16[256,768]{1,0:T(8,128)(2,1)} %copy-done.2, bf16[8192,512]{1,0:T(8,128)(2,1)} %query_ref.7, bf16[8192,128]{1,0:T(8,128)(2,1)} %key_ref.7, bf16[8192,128]{1,0:T(8,128)(2,1)} %value_ref.7), custom_call_target="tpu_custom_call" | custom-call | tf_op jit(solution)/shard_map/pallas_call | solution.py:157
  91.3 12.0 %collective-permute-done.4.right_ref = bf16[2,1024,256]{2,1,0:T(8,128)(2,1)} collective-permute-done((bf16[2,1024,256]{2,1,0:T(8,128)(2,1)}, bf16[2,1024,256]{2,1,0:T(8,128)(2,1)}, u32[]{:S(2)}, u32[]{:S(2)}) %collective-permute-start.4) | collective-permute-done | bytes 1048608 | tf_op jit(solution)/shard_map/ppermute | solution.py:281
  103.2 3.4 %collective-permute-done.3.left_ref = bf16[2,1024,256]{2,1,0:T(8,128)(2,1)} collective-permute-done((bf16[2,1024,256]{2,1,0:T(8,128)(2,1)}, bf16[2,1024,256]{2,1,0:T(8,128)(2,1)}, u32[]{:S(2)}, u32[]{:S(2)}) %collective-permute-start.3) | collective-permute-done | bytes 1048608 | tf_op jit(solution)/shard_map/ppermute | solution.py:281
  108.5 1.9 %slice.19 = bf16[1,1024,256]{2,1,0:T(8,128)(2,1)} slice(bf16[2,1024,256]{2,1,0:T(8,128)(2,1)} %collective-permute-done.4.right_ref), slice={[1:2], [0:1024], [0:256]} | slice | bytes 1048576 | tf_op jit(solution)/shard_map/slice | solution.py:336
  113.1 4.9 %collective-permute-done.8.near_ref = s16[3,272,1024]{2,1,0:T(8,128)(2,1)} collective-permute-done((s16[3,272,1024]{2,1,0:T(8,128)(2,1)}, s16[3,272,1024]{2,1,0:T(8,128)(2,1)}, u32[]{:S(2)}, u32[]{:S(2)}) %collective-permute-start.8) | collective-permute-done | bytes 1671200 | tf_op jit(solution)/shard_map/ppermute | solution.py:281
  117.9 5.8 %shard_map.114 = s16[4,272,1024]{2,1,0:T(8,128)(2,1)} custom-call(s32[3]{0:T(128)} %pad_add_fusion.2.places_ref.plan_ref, f32[3,256,1024]{2,1,0:T(8,128)} %shard_map.113.own_ref, s16[3,272,1024]{2,1,0:T(8,128)(2,1)} %collective-permute-done.8.near_ref), custom_call_target="tpu_custom_call" | custom-call | tf_op jit(solution)/shard_map/pallas_call | solution.py:181
  123.7 5.1 %all-to-all-start.2 = ((s16[4,272,1024]{2,1,0:T(8,128)(2,1)}), s16[4,272,1024]{2,1,0:T(8,128)(2,1)}, u32[]{:S(2)}, u32[]{:S(2)}) async-start(s16[4,272,1024]{2,1,0:T(8,128)(2,1)} %shard_map.114), calls=%async_computation.2 | async-start | bytes 4456448 | tf_op jit(solution)/shard_map/all_to_all | solution.py:337
  130.1 7.3 %shard_map.116 = (f32[512,768]{1,0:T(8,128)}, f32[512,768]{1,0:T(8,128)S(1)}) custom-call(s32[9]{0:T(128)S(1)} %stack.119.plan_ref, bf16[2,1024,256]{2,1,0:T(8,128)(2,1)S(1)} %copy-done, bf16[2,1024,256]{2,1,0:T(8,128)(2,1)} %collective-permute-done.4.right_ref, bf16[1,1024,256]{2,1,0:T(8,128)(2,1)} %collective-permute-done.5.far_0_ref, ...), custom_call_target="tpu_custom_call" | custom-call | tf_op jit(solution)/shard_map/pallas_call | solution.py:245
  138.5 3.3 %shard_map.115 = f32[1,256,1024]{2,1,0:T(8,128)} custom-call(s32[1]{0:T(128)} %bitcast.order_ref, bf16[256,768]{1,0:T(8,128)(2,1)} %copy-done.2, bf16[8192,512]{1,0:T(8,128)(2,1)} %query_ref.7, bf16[8192,128]{1,0:T(8,128)(2,1)} %key_ref.7, bf16[8192,128]{1,0:T(8,128)(2,1)} %value_ref.7, s16[1,272,1024]{2,1,0:T(8,128)(2,1)} %collective-permute-done.7.refs_0_), custom_call_target="tpu_custom_call" | custom-call | tf_op jit(solution)/shard_map/pallas_call | solution.py:157
  143.3 3.8 %shard_map.117 = (f32[512,512]{1,0:T(8,128)}, f32[512,128]{1,0:T(8,128)}, f32[512,128]{1,0:T(8,128)}) custom-call(f32[512,768]{1,0:T(8,128)} %copy-done.1, f32[512,768]{1,0:T(8,128)} %copy-done.3), custom_call_target="tpu_custom_call" | custom-call | tf_op jit(solution)/shard_map/pallas_call | solution.py:270
  147.1 7.4 %all-to-all-done.2.refs_0_.refs_1_.refs_2_.refs_3_.refs_4_.refs_5_ = s16[4,272,1024]{2,1,0:T(8,128)(2,1)} async-done(((s16[4,272,1024]{2,1,0:T(8,128)(2,1)}), s16[4,272,1024]{2,1,0:T(8,128)(2,1)}, u32[]{:S(2)}, u32[]{:S(2)}) %all-to-all-start.2) | async-done | bytes 2228256 | tf_op jit(solution)/shard_map/all_to_all | solution.py:337
  154.6 3.9 %shard_map.118 = f32[256,1024]{1,0:T(8,128)} custom-call(s32[3]{0:T(128)} %pad_add_fusion.2.places_ref.plan_ref, f32[256,1024]{1,0:T(8,128)} %bitcast.33, s16[4,272,1024]{2,1,0:T(8,128)(2,1)} %all-to-all-done.2.refs_0_.refs_1_.refs_2_.refs_3_.refs_4_.refs_5_, s16[4,272,1024]{2,1,0:T(8,128)(2,1)} %all-to-all-done.2.refs_0_.refs_1_.refs_2_.refs_3_.refs_4_.refs_5_, ...), custom_call_target="tpu_custom_call" | custom-call | tf_op jit(solution)/shard_map/pallas_call | solution.py:217
  (32 shorter events, 17.7 us)
Async XLA Ops:
  7.2 30.9 %all-to-all-start = ((bf16[16,32,1792]{2,1,0:T(8,128)(2,1)}), bf16[16,32,1792]{2,1,0:T(8,128)(2,1)S(1)}, u32[]{:S(2)}, u32[]{:S(2)}) async-start(bf16[16,32,1792]{2,1,0:T(8,128)(2,1)} %bitcast.31), calls=%async_computation | async-start | bytes 3670016 | tf_op jit(solution)/shard_map/all_to_all | solution.py:310
  38.5 12.2 %copy-start.2 = (bf16[256,768]{1,0:T(8,128)(2,1)}, bf16[256,768]{1,0:T(8,128)(2,1)S(1)}, u32[]{:S(2)}) copy-start(bf16[256,768]{1,0:T(8,128)(2,1)S(1)} %convolution_convert_fusion.1.rows_ref) | copy-start | bytes 1179652
  38.5 12.1 %collective-permute-start.2 = (bf16[256,768]{1,0:T(8,128)(2,1)S(1)}, bf16[256,768]{1,0:T(8,128)(2,1)S(1)}, u32[]{:S(2)}, u32[]{:S(2)}) collective-permute-start(bf16[256,768]{1,0:T(8,128)(2,1)S(1)} %convolution_convert_fusion.1.rows_ref), channel_id=1, source_target_pairs={{0,64},{64,0},{1,65},{65,1},{2,66},{66,2},{3,67},{67,3},{4,68},{68... | collective-permute-start | bytes 1179656 | tf_op jit(solution)/shard_map/ppermute | solution.py:281
  40.8 23.0 %collective-permute-start.1 = (bf16[1024,256]{1,0:T(8,128)(2,1)S(1)}, bf16[1024,256]{1,0:T(8,128)(2,1)S(1)}, u32[]{:S(2)}, u32[]{:S(2)}) collective-permute-start(bf16[1024,256]{1,0:T(8,128)(2,1)S(1)} %convolution_convert_fusion), channel_id=1, source_target_pairs={{0,1},{1,16},{2,35},{3,50},{4,68},{5,85},{6,102},{7,119},{8,9},{9,... | collective-permute-start | bytes 1572872 | tf_op jit(solution)/shard_map/ppermute | solution.py:291
  41.4 30.3 %collective-permute-start = (bf16[1024,256]{1,0:T(8,128)(2,1)S(1)}, bf16[1024,256]{1,0:T(8,128)(2,1)S(1)}, u32[]{:S(2)}, u32[]{:S(2)}) collective-permute-start(bf16[1024,256]{1,0:T(8,128)(2,1)S(1)} %convolution_convert_fusion), channel_id=1, source_target_pairs={{0,0},{1,17},{2,34},{3,51},{4,69},{5,84},{6,103},{7,118},{8,8},{9,... | collective-permute-start | bytes 1572872 | tf_op jit(solution)/shard_map/ppermute | solution.py:291
  72.7 51.0 %all-to-all-start.1 = ((bf16[4,2,256,768]{3,2,1,0:T(8,128)(2,1)}), bf16[4,2,256,768]{3,2,1,0:T(8,128)(2,1)S(1)}, u32[]{:S(2)}, u32[]{:S(2)}) async-start(bf16[4,2,256,768]{3,2,1,0:T(8,128)(2,1)} %broadcast_in_dim.2), calls=%async_computation.1 | async-start | bytes 6291456 | tf_op jit(solution)/shard_map/all_to_all | solution.py:326
  76.7 41.3 %collective-permute-start.8 = (s16[3,272,1024]{2,1,0:T(8,128)(2,1)}, s16[3,272,1024]{2,1,0:T(8,128)(2,1)}, u32[]{:S(2)}, u32[]{:S(2)}) collective-permute-start(s16[3,272,1024]{2,1,0:T(8,128)(2,1)} %get-tuple-element.36), channel_id=1, source_target_pairs={{0,1},{1,0},{2,3},{3,2},{4,5},{5,4},{6,7},{7,6},{8,9},{9,8},{10,11... | collective-permute-start | bytes 5013512 | tf_op jit(solution)/shard_map/ppermute | solution.py:281
  78.7 24.5 %collective-permute-start.4 = (bf16[2,1024,256]{2,1,0:T(8,128)(2,1)}, bf16[2,1024,256]{2,1,0:T(8,128)(2,1)}, u32[]{:S(2)}, u32[]{:S(2)}) collective-permute-start(bf16[2,1024,256]{2,1,0:T(8,128)(2,1)} %pad_maximum_fusion.pair_ref), channel_id=1, source_target_pairs={{0,6},{2,0},{4,2},{6,4},{1,7},{3,1},{5,3},{7,5},{8,14},{10,8},{12,... | collective-permute-start | bytes 3145736 | tf_op jit(solution)/shard_map/ppermute | solution.py:281
  80.7 26.0 %collective-permute-start.3 = (bf16[2,1024,256]{2,1,0:T(8,128)(2,1)}, bf16[2,1024,256]{2,1,0:T(8,128)(2,1)}, u32[]{:S(2)}, u32[]{:S(2)}) collective-permute-start(bf16[2,1024,256]{2,1,0:T(8,128)(2,1)} %pad_maximum_fusion.pair_ref), channel_id=1, source_target_pairs={{0,2},{2,4},{4,6},{6,0},{1,3},{3,5},{5,7},{7,1},{8,10},{10,12},{12... | collective-permute-start | bytes 3145736 | tf_op jit(solution)/shard_map/ppermute | solution.py:281
  80.8 48.1 %collective-permute-start.7 = (s16[1,272,1024]{2,1,0:T(8,128)(2,1)}, s16[1,272,1024]{2,1,0:T(8,128)(2,1)}, u32[]{:S(2)}, u32[]{:S(2)}) collective-permute-start(s16[1,272,1024]{2,1,0:T(8,128)(2,1)} %get-tuple-element.34), channel_id=1, source_target_pairs={{0,1},{1,0},{2,3},{3,2},{4,5},{5,4},{6,7},{7,6},{8,9},{9,8},{10,11... | collective-permute-start | bytes 1671176 | tf_op jit(solution)/shard_map/ppermute | solution.py:281
  110.4 18.5 %collective-permute-start.6 = (bf16[1,1024,256]{2,1,0:T(8,128)(2,1)}, bf16[1,1024,256]{2,1,0:T(8,128)(2,1)}, u32[]{:S(2)}, u32[]{:S(2)}) collective-permute-start(bf16[1,1024,256]{2,1,0:T(8,128)(2,1)} %slice.19), channel_id=1, source_target_pairs={{0,6},{2,0},{4,2},{6,4},{1,7},{3,1},{5,3},{7,5},{8,14},{10,8},{12,... | collective-permute-start | bytes 1572872 | tf_op jit(solution)/shard_map/ppermute | solution.py:281
  110.7 18.2 %collective-permute-start.5 = (bf16[1,1024,256]{2,1,0:T(8,128)(2,1)}, bf16[1,1024,256]{2,1,0:T(8,128)(2,1)}, u32[]{:S(2)}, u32[]{:S(2)}) collective-permute-start(bf16[1,1024,256]{2,1,0:T(8,128)(2,1)} %slice.18), channel_id=1, source_target_pairs={{0,2},{2,4},{4,6},{6,0},{1,3},{3,5},{5,7},{7,1},{8,10},{10,12},{12... | collective-permute-start | bytes 1572872 | tf_op jit(solution)/shard_map/ppermute | solution.py:281
  123.7 30.9 %all-to-all-start.2 = ((s16[4,272,1024]{2,1,0:T(8,128)(2,1)}), s16[4,272,1024]{2,1,0:T(8,128)(2,1)}, u32[]{:S(2)}, u32[]{:S(2)}) async-start(s16[4,272,1024]{2,1,0:T(8,128)(2,1)} %shard_map.114), calls=%async_computation.2 | async-start | bytes 4456448 | tf_op jit(solution)/shard_map/all_to_all | solution.py:337
  128.9 1.2 copy-start
  137.4 1.2 copy-start.1
  138.5 3.6 %collective-permute-start.9 = (f32[512,768]{1,0:T(8,128)}, f32[512,768]{1,0:T(8,128)S(1)}, u32[]{:S(2)}, u32[]{:S(2)}) collective-permute-start(f32[512,768]{1,0:T(8,128)} %get-tuple-element.42), channel_id=1, source_target_pairs={{0,8},{8,0},{1,9},{9,1},{2,10},{10,2},{3,11},{11,3},{4,12},{12,4},... | collective-permute-start | bytes 4718600 | tf_op jit(solution)/shard_map/ppermute | solution.py:281
  142.2 1.1 copy-start.3

commit v4 on v2

--- a/solution.py
+++ b/solution.py
@@ -25,10 +25,12 @@
 
 def pack_kernel(per_pair, me_ref, slots_ref, *refs):
     *value_refs, out_ref = refs
-    slots = slots_ref[...]
     me = me_ref[0]
-    count, width = slots.shape
     capacity = value_refs[0].shape[0]
+    count = capacity // per_pair
+    parts = slots_ref.shape[0] // count
+    slots = jnp.concatenate([slots_ref[pl.ds(i, count, parts), :] for i in range(parts)], axis=1)
+    width = slots.shape[1]
     first_row = me * capacity
     lead = slots[:1, :]
     before = jnp.sum((lead < first_row).astype(jnp.float32)).astype(jnp.int32)
@@ -54,10 +56,10 @@
         first += ref.shape[1]
 
 
-def pack_rows(source, my_index, dp_count, per_pair, values):
+def pack_rows(source, my_index, per_pair, values):
     capacity = values[0].shape[0]
     width = sum(v.shape[1] for v in values)
-    slots = source.reshape(dp_count, -1)
+    slots = source.reshape(-1, 128)
     whole = lambda shape: pl.BlockSpec(shape, lambda g, me_ref: (0, 0))
     return pl.pallas_call(
         functools.partial(pack_kernel, per_pair),
@@ -292,7 +294,7 @@
     width = query_width + 2 * key_width
     flat_slots = balanced_slots(source, dp_count, per_pair)
 
-    packed = pack_rows(source, my_index, dp_count, per_pair, (normed, query_back, key_back, value_back))
+    packed = pack_rows(source, my_index, per_pair, (normed, query_back, key_back, value_back))
     packed = packed.reshape(dp_count, per_pair, -1)
     relayed = lax.all_to_all(packed, DP, split_axis=0, concat_axis=0, tiled=True).reshape(capacity, -1)
     back_mine = take_rows(relayed[:, features:], flat_slots)

time: 159 us -> 157 us (0.987)
  no operation moved by 1% of the time
where the time goes in v4:
time: 157 us; the launch traced here: 156 us
  waiting for transfers between devices  64.1 us (41%)
  Pallas kernels  42.8 us (27%)
  starting transfers between devices  33.9 us (22%)
  local copies, waits for them, and re-layouts  9.23 us (6%)
  other arithmetic  4.56 us (3%)
    ppermute x8, waiting for transfers between devices, shifted(): lax.ppermute(values, axis, [(i, (i + by) % size) for i in range(size)])  22.8 us
    all_to_all x1, waiting for transfers between devices, body(): lax.all_to_all(packed, DP, split_axis=0, concat_axis=0, tiled=True)  22.5 us
    pallas_call x3, Pallas kernels, partials(): pl.pallas_call(functools.partial(partial_kernel, sizes, len(arrived), cod...  17.7 us
    ppermute x2, waiting for transfers between devices, to_feature_owner(): return lax.ppermute(values, DP + TENSOR, pairs)  11.4 us
    ppermute x8, starting transfers between devices, shifted(): lax.ppermute(values, axis, [(i, (i + by) % size) for i in range(size)])  11.2 us
    all_to_all x1, waiting for transfers between devices, body(): lax.all_to_all(to_others, 'x', split_axis=0, concat_axis=0, tiled=True)  7.42 us
    pallas_call x1, Pallas kernels, weight_halves(): pl.pallas_call(weight_kernel, grid_spec=pltpu.PrefetchScalarGridSpec(num_...  7.25 us
    ppermute x2, starting transfers between devices, to_feature_owner(): return lax.ppermute(values, DP + TENSOR, pairs)  6.83 us
  transfers between devices with their start and end apart: 13, of which 9 were waited for; matrix products, arithmetic and copies ran while one was open for 6% of the time, Pallas kernels for 22%

profile of v4, /device:TPU:24, one launch (start us, length us, event | category | flops | bytes accessed | tf_op | source)
XLA Modules:
  0.0 156.3 jit_solution(15724279478077045389)
XLA Ops:
  0.6 4.3 %shard_map.111 = bf16[512,1792]{1,0:T(8,128)(2,1)} custom-call(s32[1]{0:T(128)} %bitcast.1.me_ref, s32[32,128]{1,0:T(8,128)} %bitcast.39, bf16[512,1024]{1,0:T(8,128)(2,1)} %refs_0_.1, bf16[512,512]{1,0:T(8,128)(2,1)} %refs_1_.1, bf16[512,128]{1,0:T(8,128)(2,1)} %refs_2_.1, bf16[512,128]{1,0:T(8,128)(2,1)} %refs_3_.1), custom_call_target="tpu_custom_call" | custom-call | tf_op jit(solution)/shard_map/pallas_call | solution.py:64
  5.0 6.8 %all-to-all-start = ((bf16[16,32,1792]{2,1,0:T(8,128)(2,1)}), bf16[16,32,1792]{2,1,0:T(8,128)(2,1)S(1)}, u32[]{:S(2)}, u32[]{:S(2)}) async-start(bf16[16,32,1792]{2,1,0:T(8,128)(2,1)} %bitcast.31), calls=%async_computation | async-start | bytes 3670016 | tf_op jit(solution)/shard_map/all_to_all | solution.py:299
  13.4 22.5 %all-to-all-done = bf16[16,32,1792]{2,1,0:T(8,128)(2,1)S(1)} async-done(((bf16[16,32,1792]{2,1,0:T(8,128)(2,1)}), bf16[16,32,1792]{2,1,0:T(8,128)(2,1)S(1)}, u32[]{:S(2)}, u32[]{:S(2)}) %all-to-all-start) | async-done | bytes 1835040 | tf_op jit(solution)/shard_map/all_to_all | solution.py:299
  39.2 6.2 %collective-permute-start = (bf16[1024,256]{1,0:T(8,128)(2,1)S(1)}, bf16[1024,256]{1,0:T(8,128)(2,1)S(1)}, u32[]{:S(2)}, u32[]{:S(2)}) collective-permute-start(bf16[1024,256]{1,0:T(8,128)(2,1)S(1)} %convolution_convert_fusion), channel_id=1, source_target_pairs={{0,0},{1,17},{2,34},{3,51},{4,69},{5,84},{6,103},{7,118},{8,8},{9,... | collective-permute-start | bytes 1572872 | tf_op jit(solution)/shard_map/ppermute | solution.py:280
  46.1 2.3 %collective-permute-done.2 = bf16[256,768]{1,0:T(8,128)(2,1)S(1)} collective-permute-done((bf16[256,768]{1,0:T(8,128)(2,1)S(1)}, bf16[256,768]{1,0:T(8,128)(2,1)S(1)}, u32[]{:S(2)}, u32[]{:S(2)}) %collective-permute-start.2) | collective-permute-done | bytes 393248 | tf_op jit(solution)/shard_map/ppermute | solution.py:270
  50.3 7.7 %shard_map.112 = (s16[3,272,1024]{2,1,0:T(8,128)(2,1)}, s16[1,272,1024]{2,1,0:T(8,128)(2,1)}) custom-call(s32[4]{0:T(128)} %pad_add_fusion.order_ref, bf16[256,768]{1,0:T(8,128)(2,1)} %copy-done.2, bf16[8192,512]{1,0:T(8,128)(2,1)} %query_ref.5, bf16[8192,128]{1,0:T(8,128)(2,1)} %key_ref.5, bf16[8192,128]{1,0:T(8,128)(2,1)} %value_ref.5), custom_call_target="tpu_custom_call" | custom-call | tf_op jit(solution)/shard_map/pallas_call | solution.py:146
  58.1 3.4 %collective-permute-done.1 = bf16[1024,256]{1,0:T(8,128)(2,1)S(1)} collective-permute-done((bf16[1024,256]{1,0:T(8,128)(2,1)S(1)}, bf16[1024,256]{1,0:T(8,128)(2,1)S(1)}, u32[]{:S(2)}, u32[]{:S(2)}) %collective-permute-start.1) | collective-permute-done | bytes 524320 | tf_op jit(solution)/shard_map/ppermute | solution.py:280
  61.5 7.9 %collective-permute-done = bf16[1024,256]{1,0:T(8,128)(2,1)S(1)} collective-permute-done((bf16[1024,256]{1,0:T(8,128)(2,1)S(1)}, bf16[1024,256]{1,0:T(8,128)(2,1)S(1)}, u32[]{:S(2)}, u32[]{:S(2)}) %collective-permute-start) | collective-permute-done | bytes 524320 | tf_op jit(solution)/shard_map/ppermute | solution.py:280
  70.5 3.9 %all-to-all-start.1 = ((bf16[4,2,256,768]{3,2,1,0:T(8,128)(2,1)}), bf16[4,2,256,768]{3,2,1,0:T(8,128)(2,1)S(1)}, u32[]{:S(2)}, u32[]{:S(2)}) async-start(bf16[4,2,256,768]{3,2,1,0:T(8,128)(2,1)} %broadcast_in_dim.2), calls=%async_computation.1 | async-start | bytes 6291456 | tf_op jit(solution)/shard_map/all_to_all | solution.py:315
  74.5 2.1 %collective-permute-start.8 = (s16[3,272,1024]{2,1,0:T(8,128)(2,1)}, s16[3,272,1024]{2,1,0:T(8,128)(2,1)}, u32[]{:S(2)}, u32[]{:S(2)}) collective-permute-start(s16[3,272,1024]{2,1,0:T(8,128)(2,1)} %get-tuple-element.36), channel_id=1, source_target_pairs={{0,1},{1,0},{2,3},{3,2},{4,5},{5,4},{6,7},{7,6},{8,9},{9,8},{10,11... | collective-permute-start | bytes 5013512 | tf_op jit(solution)/shard_map/ppermute | solution.py:270
  76.5 1.9 %collective-permute-start.4 = (bf16[2,1024,256]{2,1,0:T(8,128)(2,1)}, bf16[2,1024,256]{2,1,0:T(8,128)(2,1)}, u32[]{:S(2)}, u32[]{:S(2)}) collective-permute-start(bf16[2,1024,256]{2,1,0:T(8,128)(2,1)} %pad_maximum_fusion.pair_ref), channel_id=1, source_target_pairs={{0,6},{2,0},{4,2},{6,4},{1,7},{3,1},{5,3},{7,5},{8,14},{10,8},{12,... | collective-permute-start | bytes 3145736 | tf_op jit(solution)/shard_map/ppermute | solution.py:270
  78.6 3.4 %collective-permute-start.7 = (s16[1,272,1024]{2,1,0:T(8,128)(2,1)}, s16[1,272,1024]{2,1,0:T(8,128)(2,1)}, u32[]{:S(2)}, u32[]{:S(2)}) collective-permute-start(s16[1,272,1024]{2,1,0:T(8,128)(2,1)} %get-tuple-element.34), channel_id=1, source_target_pairs={{0,1},{1,0},{2,3},{3,2},{4,5},{5,4},{6,7},{7,6},{8,9},{9,8},{10,11... | collective-permute-start | bytes 1671176 | tf_op jit(solution)/shard_map/ppermute | solution.py:270
  82.5 6.6 %shard_map.113.own_ref = f32[3,256,1024]{2,1,0:T(8,128)} custom-call(s32[3]{0:T(128)} %pad_add_fusion.1.order_ref, bf16[256,768]{1,0:T(8,128)(2,1)} %copy-done.2, bf16[8192,512]{1,0:T(8,128)(2,1)} %query_ref.5, bf16[8192,128]{1,0:T(8,128)(2,1)} %key_ref.5, bf16[8192,128]{1,0:T(8,128)(2,1)} %value_ref.5), custom_call_target="tpu_custom_call" | custom-call | tf_op jit(solution)/shard_map/pallas_call | solution.py:146
  89.1 12.0 %collective-permute-done.4.right_ref = bf16[2,1024,256]{2,1,0:T(8,128)(2,1)} collective-permute-done((bf16[2,1024,256]{2,1,0:T(8,128)(2,1)}, bf16[2,1024,256]{2,1,0:T(8,128)(2,1)}, u32[]{:S(2)}, u32[]{:S(2)}) %collective-permute-start.4) | collective-permute-done | bytes 1048608 | tf_op jit(solution)/shard_map/ppermute | solution.py:270
  101.1 3.4 %collective-permute-done.3.left_ref = bf16[2,1024,256]{2,1,0:T(8,128)(2,1)} collective-permute-done((bf16[2,1024,256]{2,1,0:T(8,128)(2,1)}, bf16[2,1024,256]{2,1,0:T(8,128)(2,1)}, u32[]{:S(2)}, u32[]{:S(2)}) %collective-permute-start.3) | collective-permute-done | bytes 1048608 | tf_op jit(solution)/shard_map/ppermute | solution.py:270
  106.3 1.9 %slice.19 = bf16[1,1024,256]{2,1,0:T(8,128)(2,1)} slice(bf16[2,1024,256]{2,1,0:T(8,128)(2,1)} %collective-permute-done.4.right_ref), slice={[1:2], [0:1024], [0:256]} | slice | bytes 1048576 | tf_op jit(solution)/shard_map/slice | solution.py:325
  110.9 4.9 %collective-permute-done.8.near_ref = s16[3,272,1024]{2,1,0:T(8,128)(2,1)} collective-permute-done((s16[3,272,1024]{2,1,0:T(8,128)(2,1)}, s16[3,272,1024]{2,1,0:T(8,128)(2,1)}, u32[]{:S(2)}, u32[]{:S(2)}) %collective-permute-start.8) | collective-permute-done | bytes 1671200 | tf_op jit(solution)/shard_map/ppermute | solution.py:270
  115.7 5.8 %shard_map.114 = s16[4,272,1024]{2,1,0:T(8,128)(2,1)} custom-call(s32[3]{0:T(128)} %pad_add_fusion.2.places_ref.plan_ref, f32[3,256,1024]{2,1,0:T(8,128)} %shard_map.113.own_ref, s16[3,272,1024]{2,1,0:T(8,128)(2,1)} %collective-permute-done.8.near_ref), custom_call_target="tpu_custom_call" | custom-call | tf_op jit(solution)/shard_map/pallas_call | solution.py:170
  121.5 5.1 %all-to-all-start.2 = ((s16[4,272,1024]{2,1,0:T(8,128)(2,1)}), s16[4,272,1024]{2,1,0:T(8,128)(2,1)}, u32[]{:S(2)}, u32[]{:S(2)}) async-start(s16[4,272,1024]{2,1,0:T(8,128)(2,1)} %shard_map.114), calls=%async_computation.2 | async-start | bytes 4456448 | tf_op jit(solution)/shard_map/all_to_all | solution.py:326
  127.9 7.3 %shard_map.116 = (f32[512,768]{1,0:T(8,128)}, f32[512,768]{1,0:T(8,128)S(1)}) custom-call(s32[9]{0:T(128)S(1)} %stack.119.plan_ref, bf16[2,1024,256]{2,1,0:T(8,128)(2,1)S(1)} %copy-done, bf16[2,1024,256]{2,1,0:T(8,128)(2,1)} %collective-permute-done.4.right_ref, bf16[1,1024,256]{2,1,0:T(8,128)(2,1)} %collective-permute-done.5.far_0_ref, ...), custom_call_target="tpu_custom_call" | custom-call | tf_op jit(solution)/shard_map/pallas_call | solution.py:234
  136.4 3.3 %shard_map.115 = f32[1,256,1024]{2,1,0:T(8,128)} custom-call(s32[1]{0:T(128)} %bitcast.order_ref, bf16[256,768]{1,0:T(8,128)(2,1)} %copy-done.2, bf16[8192,512]{1,0:T(8,128)(2,1)} %query_ref.5, bf16[8192,128]{1,0:T(8,128)(2,1)} %key_ref.5, bf16[8192,128]{1,0:T(8,128)(2,1)} %value_ref.5, s16[1,272,1024]{2,1,0:T(8,128)(2,1)} %collective-permute-done.7.refs_0_), custom_call_target="tpu_custom_call" | custom-call | tf_op jit(solution)/shard_map/pallas_call | solution.py:146
  141.1 3.8 %shard_map.117 = (f32[512,512]{1,0:T(8,128)}, f32[512,128]{1,0:T(8,128)}, f32[512,128]{1,0:T(8,128)}) custom-call(f32[512,768]{1,0:T(8,128)} %copy-done.1, f32[512,768]{1,0:T(8,128)} %copy-done.3), custom_call_target="tpu_custom_call" | custom-call | tf_op jit(solution)/shard_map/pallas_call | solution.py:259
  145.0 7.4 %all-to-all-done.2.refs_0_.refs_1_.refs_2_.refs_3_.refs_4_.refs_5_ = s16[4,272,1024]{2,1,0:T(8,128)(2,1)} async-done(((s16[4,272,1024]{2,1,0:T(8,128)(2,1)}), s16[4,272,1024]{2,1,0:T(8,128)(2,1)}, u32[]{:S(2)}, u32[]{:S(2)}) %all-to-all-start.2) | async-done | bytes 2228256 | tf_op jit(solution)/shard_map/all_to_all | solution.py:326
  152.4 3.9 %shard_map.118 = f32[256,1024]{1,0:T(8,128)} custom-call(s32[3]{0:T(128)} %pad_add_fusion.2.places_ref.plan_ref, f32[256,1024]{1,0:T(8,128)} %bitcast.33, s16[4,272,1024]{2,1,0:T(8,128)(2,1)} %all-to-all-done.2.refs_0_.refs_1_.refs_2_.refs_3_.refs_4_.refs_5_, s16[4,272,1024]{2,1,0:T(8,128)(2,1)} %all-to-all-done.2.refs_0_.refs_1_.refs_2_.refs_3_.refs_4_.refs_5_, ...), custom_call_target="tpu_custom_call" | custom-call | tf_op jit(solution)/shard_map/pallas_call | solution.py:206
  (32 shorter events, 17.7 us)
Async XLA Ops:
  5.0 30.9 %all-to-all-start = ((bf16[16,32,1792]{2,1,0:T(8,128)(2,1)}), bf16[16,32,1792]{2,1,0:T(8,128)(2,1)S(1)}, u32[]{:S(2)}, u32[]{:S(2)}) async-start(bf16[16,32,1792]{2,1,0:T(8,128)(2,1)} %bitcast.31), calls=%async_computation | async-start | bytes 3670016 | tf_op jit(solution)/shard_map/all_to_all | solution.py:299
  36.3 12.2 %copy-start.2 = (bf16[256,768]{1,0:T(8,128)(2,1)}, bf16[256,768]{1,0:T(8,128)(2,1)S(1)}, u32[]{:S(2)}) copy-start(bf16[256,768]{1,0:T(8,128)(2,1)S(1)} %convolution_convert_fusion.1.rows_ref) | copy-start | bytes 1179652
  36.3 12.1 %collective-permute-start.2 = (bf16[256,768]{1,0:T(8,128)(2,1)S(1)}, bf16[256,768]{1,0:T(8,128)(2,1)S(1)}, u32[]{:S(2)}, u32[]{:S(2)}) collective-permute-start(bf16[256,768]{1,0:T(8,128)(2,1)S(1)} %convolution_convert_fusion.1.rows_ref), channel_id=1, source_target_pairs={{0,64},{64,0},{1,65},{65,1},{2,66},{66,2},{3,67},{67,3},{4,68},{68... | collective-permute-start | bytes 1179656 | tf_op jit(solution)/shard_map/ppermute | solution.py:270
  38.6 23.0 %collective-permute-start.1 = (bf16[1024,256]{1,0:T(8,128)(2,1)S(1)}, bf16[1024,256]{1,0:T(8,128)(2,1)S(1)}, u32[]{:S(2)}, u32[]{:S(2)}) collective-permute-start(bf16[1024,256]{1,0:T(8,128)(2,1)S(1)} %convolution_convert_fusion), channel_id=1, source_target_pairs={{0,1},{1,16},{2,35},{3,50},{4,68},{5,85},{6,102},{7,119},{8,9},{9,... | collective-permute-start | bytes 1572872 | tf_op jit(solution)/shard_map/ppermute | solution.py:280
  39.2 30.3 %collective-permute-start = (bf16[1024,256]{1,0:T(8,128)(2,1)S(1)}, bf16[1024,256]{1,0:T(8,128)(2,1)S(1)}, u32[]{:S(2)}, u32[]{:S(2)}) collective-permute-start(bf16[1024,256]{1,0:T(8,128)(2,1)S(1)} %convolution_convert_fusion), channel_id=1, source_target_pairs={{0,0},{1,17},{2,34},{3,51},{4,69},{5,84},{6,103},{7,118},{8,8},{9,... | collective-permute-start | bytes 1572872 | tf_op jit(solution)/shard_map/ppermute | solution.py:280
  70.5 50.9 %all-to-all-start.1 = ((bf16[4,2,256,768]{3,2,1,0:T(8,128)(2,1)}), bf16[4,2,256,768]{3,2,1,0:T(8,128)(2,1)S(1)}, u32[]{:S(2)}, u32[]{:S(2)}) async-start(bf16[4,2,256,768]{3,2,1,0:T(8,128)(2,1)} %broadcast_in_dim.2), calls=%async_computation.1 | async-start | bytes 6291456 | tf_op jit(solution)/shard_map/all_to_all | solution.py:315
  74.5 41.3 %collective-permute-start.8 = (s16[3,272,1024]{2,1,0:T(8,128)(2,1)}, s16[3,272,1024]{2,1,0:T(8,128)(2,1)}, u32[]{:S(2)}, u32[]{:S(2)}) collective-permute-start(s16[3,272,1024]{2,1,0:T(8,128)(2,1)} %get-tuple-element.36), channel_id=1, source_target_pairs={{0,1},{1,0},{2,3},{3,2},{4,5},{5,4},{6,7},{7,6},{8,9},{9,8},{10,11... | collective-permute-start | bytes 5013512 | tf_op jit(solution)/shard_map/ppermute | solution.py:270
  76.5 24.5 %collective-permute-start.4 = (bf16[2,1024,256]{2,1,0:T(8,128)(2,1)}, bf16[2,1024,256]{2,1,0:T(8,128)(2,1)}, u32[]{:S(2)}, u32[]{:S(2)}) collective-permute-start(bf16[2,1024,256]{2,1,0:T(8,128)(2,1)} %pad_maximum_fusion.pair_ref), channel_id=1, source_target_pairs={{0,6},{2,0},{4,2},{6,4},{1,7},{3,1},{5,3},{7,5},{8,14},{10,8},{12,... | collective-permute-start | bytes 3145736 | tf_op jit(solution)/shard_map/ppermute | solution.py:270
  78.5 26.0 %collective-permute-start.3 = (bf16[2,1024,256]{2,1,0:T(8,128)(2,1)}, bf16[2,1024,256]{2,1,0:T(8,128)(2,1)}, u32[]{:S(2)}, u32[]{:S(2)}) collective-permute-start(bf16[2,1024,256]{2,1,0:T(8,128)(2,1)} %pad_maximum_fusion.pair_ref), channel_id=1, source_target_pairs={{0,2},{2,4},{4,6},{6,0},{1,3},{3,5},{5,7},{7,1},{8,10},{10,12},{12... | collective-permute-start | bytes 3145736 | tf_op jit(solution)/shard_map/ppermute | solution.py:270
  78.6 48.1 %collective-permute-start.7 = (s16[1,272,1024]{2,1,0:T(8,128)(2,1)}, s16[1,272,1024]{2,1,0:T(8,128)(2,1)}, u32[]{:S(2)}, u32[]{:S(2)}) collective-permute-start(s16[1,272,1024]{2,1,0:T(8,128)(2,1)} %get-tuple-element.34), channel_id=1, source_target_pairs={{0,1},{1,0},{2,3},{3,2},{4,5},{5,4},{6,7},{7,6},{8,9},{9,8},{10,11... | collective-permute-start | bytes 1671176 | tf_op jit(solution)/shard_map/ppermute | solution.py:270
  108.2 18.5 %collective-permute-start.6 = (bf16[1,1024,256]{2,1,0:T(8,128)(2,1)}, bf16[1,1024,256]{2,1,0:T(8,128)(2,1)}, u32[]{:S(2)}, u32[]{:S(2)}) collective-permute-start(bf16[1,1024,256]{2,1,0:T(8,128)(2,1)} %slice.19), channel_id=1, source_target_pairs={{0,6},{2,0},{4,2},{6,4},{1,7},{3,1},{5,3},{7,5},{8,14},{10,8},{12,... | collective-permute-start | bytes 1572872 | tf_op jit(solution)/shard_map/ppermute | solution.py:270
  108.5 18.2 %collective-permute-start.5 = (bf16[1,1024,256]{2,1,0:T(8,128)(2,1)}, bf16[1,1024,256]{2,1,0:T(8,128)(2,1)}, u32[]{:S(2)}, u32[]{:S(2)}) collective-permute-start(bf16[1,1024,256]{2,1,0:T(8,128)(2,1)} %slice.18), channel_id=1, source_target_pairs={{0,2},{2,4},{4,6},{6,0},{1,3},{3,5},{5,7},{7,1},{8,10},{10,12},{12... | collective-permute-start | bytes 1572872 | tf_op jit(solution)/shard_map/ppermute | solution.py:270
  121.5 30.9 %all-to-all-start.2 = ((s16[4,272,1024]{2,1,0:T(8,128)(2,1)}), s16[4,272,1024]{2,1,0:T(8,128)(2,1)}, u32[]{:S(2)}, u32[]{:S(2)}) async-start(s16[4,272,1024]{2,1,0:T(8,128)(2,1)} %shard_map.114), calls=%async_computation.2 | async-start | bytes 4456448 | tf_op jit(solution)/shard_map/all_to_all | solution.py:326
  126.7 1.2 copy-start
  135.2 1.2 copy-start.1
  136.4 3.6 %collective-permute-start.9 = (f32[512,768]{1,0:T(8,128)}, f32[512,768]{1,0:T(8,128)S(1)}, u32[]{:S(2)}, u32[]{:S(2)}) collective-permute-start(f32[512,768]{1,0:T(8,128)} %get-tuple-element.42), channel_id=1, source_target_pairs={{0,8},{8,0},{1,9},{9,1},{2,10},{10,2},{3,11},{11,3},{4,12},{12,4},... | collective-permute-start | bytes 4718600 | tf_op jit(solution)/shard_map/ppermute | solution.py:270
  140.0 1.1 copy-start.3

commit v5 on v4

--- a/solution.py
+++ b/solution.py
@@ -179,7 +179,7 @@
             out_specs=pl.BlockSpec(coded_block, lambda g, places_ref: (places_ref[g], 0, 0)),
         ),
         out_shape=jax.ShapeDtypeStruct((blocks + 1,) + coded_block[1:], jnp.int16),
-        compiler_params=pltpu.CompilerParams(vmem_limit_bytes=56 * 2**20),
+        compiler_params=pltpu.CompilerParams(vmem_limit_bytes=28 * 2**20),
     )(places, own, near)
 
 

time: 157 us -> 159 us (1.013)
  local copies, waits for them, and re-layouts: 9.23 us -> 12.6 us
  Pallas kernels: 42.8 us -> 40.7 us
    unnamed x8 -> x14, local copies, waits for them, and re-layouts: 3.53 us -> 6.93 us
    pallas_call x1, Pallas kernels: 5.76 us -> 3.68 us  [recoded(): pl.pallas_call(recode_kernel, grid_spec=pltpu.PrefetchScalarGridSpec(num_...]
  transfers between devices with their start and end apart: 13 -> 13, of which waited for: 9 -> 9; matrix products, arithmetic and copies ran while one was open for 6% -> 6% of each run, Pallas kernels for 22% -> 21%
where the time goes in v5:
time: 159 us; the launch traced here: 158 us
  waiting for transfers between devices  64.7 us (41%)
  Pallas kernels  40.7 us (26%)
  starting transfers between devices  34 us (21%)
  local copies, waits for them, and re-layouts  12.6 us (8%)
  other arithmetic  3.93 us (2%)
    ppermute x8, waiting for transfers between devices, shifted(): lax.ppermute(values, axis, [(i, (i + by) % size) for i in range(size)])  23.5 us
    all_to_all x1, waiting for transfers between devices, body(): lax.all_to_all(packed, DP, split_axis=0, concat_axis=0, tiled=True)  22.5 us
    pallas_call x3, Pallas kernels, partials(): pl.pallas_call(functools.partial(partial_kernel, sizes, len(arrived), cod...  17.6 us
    ppermute x2, waiting for transfers between devices, to_feature_owner(): return lax.ppermute(values, DP + TENSOR, pairs)  11.4 us
    ppermute x8, starting transfers between devices, shifted(): lax.ppermute(values, axis, [(i, (i + by) % size) for i in range(size)])  11.3 us
    pallas_call x1, Pallas kernels, weight_halves(): pl.pallas_call(weight_kernel, grid_spec=pltpu.PrefetchScalarGridSpec(num_...  7.31 us
    all_to_all x1, waiting for transfers between devices, body(): lax.all_to_all(to_others, 'x', split_axis=0, concat_axis=0, tiled=True)  7.26 us
    unnamed x14, local copies, waits for them, and re-layouts  6.93 us
  transfers between devices with their start and end apart: 13, of which 9 were waited for; matrix products, arithmetic and copies ran while one was open for 6% of the time, Pallas kernels for 21%

profile of v5, /device:TPU:24, one launch (start us, length us, event | category | flops | bytes accessed | tf_op | source)
XLA Modules:
  0.0 157.7 jit_solution(16926399701321514192)
XLA Ops:
  0.6 4.4 %shard_map.111 = bf16[512,1792]{1,0:T(8,128)(2,1)} custom-call(s32[1]{0:T(128)} %bitcast.1.me_ref, s32[32,128]{1,0:T(8,128)} %bitcast.39, bf16[512,1024]{1,0:T(8,128)(2,1)} %refs_0_.1, bf16[512,512]{1,0:T(8,128)(2,1)} %refs_1_.1, bf16[512,128]{1,0:T(8,128)(2,1)} %refs_2_.1, bf16[512,128]{1,0:T(8,128)(2,1)} %refs_3_.1), custom_call_target="tpu_custom_call" | custom-call | tf_op jit(solution)/shard_map/pallas_call | solution.py:64
  5.0 6.8 %all-to-all-start = ((bf16[16,32,1792]{2,1,0:T(8,128)(2,1)}), bf16[16,32,1792]{2,1,0:T(8,128)(2,1)S(1)}, u32[]{:S(2)}, u32[]{:S(2)}) async-start(bf16[16,32,1792]{2,1,0:T(8,128)(2,1)} %bitcast.31), calls=%async_computation | async-start | bytes 3670016 | tf_op jit(solution)/shard_map/all_to_all | solution.py:299
  13.4 22.5 %all-to-all-done = bf16[16,32,1792]{2,1,0:T(8,128)(2,1)S(1)} async-done(((bf16[16,32,1792]{2,1,0:T(8,128)(2,1)}), bf16[16,32,1792]{2,1,0:T(8,128)(2,1)S(1)}, u32[]{:S(2)}, u32[]{:S(2)}) %all-to-all-start) | async-done | bytes 1835040 | tf_op jit(solution)/shard_map/all_to_all | solution.py:299
  39.3 6.2 %collective-permute-start = (bf16[1024,256]{1,0:T(8,128)(2,1)S(1)}, bf16[1024,256]{1,0:T(8,128)(2,1)S(1)}, u32[]{:S(2)}, u32[]{:S(2)}) collective-permute-start(bf16[1024,256]{1,0:T(8,128)(2,1)S(1)} %convolution_convert_fusion), channel_id=1, source_target_pairs={{0,0},{1,17},{2,34},{3,51},{4,69},{5,84},{6,103},{7,118},{8,8},{9,... | collective-permute-start | bytes 1572872 | tf_op jit(solution)/shard_map/ppermute | solution.py:280
  46.1 2.3 %collective-permute-done.2 = bf16[256,768]{1,0:T(8,128)(2,1)S(1)} collective-permute-done((bf16[256,768]{1,0:T(8,128)(2,1)S(1)}, bf16[256,768]{1,0:T(8,128)(2,1)S(1)}, u32[]{:S(2)}, u32[]{:S(2)}) %collective-permute-start.2) | collective-permute-done | bytes 393248 | tf_op jit(solution)/shard_map/ppermute | solution.py:270
  50.4 7.7 %shard_map.112 = (s16[3,272,1024]{2,1,0:T(8,128)(2,1)}, s16[1,272,1024]{2,1,0:T(8,128)(2,1)}) custom-call(s32[4]{0:T(128)} %pad_add_fusion.order_ref, bf16[256,768]{1,0:T(8,128)(2,1)} %copy-done.5, bf16[8192,512]{1,0:T(8,128)(2,1)} %query_ref.5, bf16[8192,128]{1,0:T(8,128)(2,1)} %key_ref.5, bf16[8192,128]{1,0:T(8,128)(2,1)} %value_ref.5), custom_call_target="tpu_custom_call" | custom-call | tf_op jit(solution)/shard_map/pallas_call | solution.py:146
  58.1 3.5 %collective-permute-done.1 = bf16[1024,256]{1,0:T(8,128)(2,1)S(1)} collective-permute-done((bf16[1024,256]{1,0:T(8,128)(2,1)S(1)}, bf16[1024,256]{1,0:T(8,128)(2,1)S(1)}, u32[]{:S(2)}, u32[]{:S(2)}) %collective-permute-start.1) | collective-permute-done | bytes 524320 | tf_op jit(solution)/shard_map/ppermute | solution.py:280
  61.6 7.9 %collective-permute-done = bf16[1024,256]{1,0:T(8,128)(2,1)S(1)} collective-permute-done((bf16[1024,256]{1,0:T(8,128)(2,1)S(1)}, bf16[1024,256]{1,0:T(8,128)(2,1)S(1)}, u32[]{:S(2)}, u32[]{:S(2)}) %collective-permute-start) | collective-permute-done | bytes 524320 | tf_op jit(solution)/shard_map/ppermute | solution.py:280
  70.6 3.9 %all-to-all-start.1 = ((bf16[4,2,256,768]{3,2,1,0:T(8,128)(2,1)}), bf16[4,2,256,768]{3,2,1,0:T(8,128)(2,1)S(1)}, u32[]{:S(2)}, u32[]{:S(2)}) async-start(bf16[4,2,256,768]{3,2,1,0:T(8,128)(2,1)} %broadcast_in_dim.2), calls=%async_computation.1 | async-start | bytes 6291456 | tf_op jit(solution)/shard_map/all_to_all | solution.py:315
  74.5 2.1 %collective-permute-start.8 = (s16[3,272,1024]{2,1,0:T(8,128)(2,1)}, s16[3,272,1024]{2,1,0:T(8,128)(2,1)}, u32[]{:S(2)}, u32[]{:S(2)}) collective-permute-start(s16[3,272,1024]{2,1,0:T(8,128)(2,1)} %get-tuple-element.36), channel_id=1, source_target_pairs={{0,1},{1,0},{2,3},{3,2},{4,5},{5,4},{6,7},{7,6},{8,9},{9,8},{10,11... | collective-permute-start | bytes 5013512 | tf_op jit(solution)/shard_map/ppermute | solution.py:270
  76.6 1.9 %collective-permute-start.4 = (bf16[2,1024,256]{2,1,0:T(8,128)(2,1)}, bf16[2,1024,256]{2,1,0:T(8,128)(2,1)}, u32[]{:S(2)}, u32[]{:S(2)}) collective-permute-start(bf16[2,1024,256]{2,1,0:T(8,128)(2,1)} %pad_maximum_fusion.pair_ref), channel_id=1, source_target_pairs={{0,6},{2,0},{4,2},{6,4},{1,7},{3,1},{5,3},{7,5},{8,14},{10,8},{12,... | collective-permute-start | bytes 3145736 | tf_op jit(solution)/shard_map/ppermute | solution.py:270
  78.6 3.4 %collective-permute-start.7 = (s16[1,272,1024]{2,1,0:T(8,128)(2,1)}, s16[1,272,1024]{2,1,0:T(8,128)(2,1)}, u32[]{:S(2)}, u32[]{:S(2)}) collective-permute-start(s16[1,272,1024]{2,1,0:T(8,128)(2,1)} %get-tuple-element.34), channel_id=1, source_target_pairs={{0,1},{1,0},{2,3},{3,2},{4,5},{5,4},{6,7},{7,6},{8,9},{9,8},{10,11... | collective-permute-start | bytes 1671176 | tf_op jit(solution)/shard_map/ppermute | solution.py:270
  82.5 6.6 %shard_map.113.own_ref = f32[3,256,1024]{2,1,0:T(8,128)} custom-call(s32[3]{0:T(128)} %pad_add_fusion.1.order_ref, bf16[256,768]{1,0:T(8,128)(2,1)} %copy-done.5, bf16[8192,512]{1,0:T(8,128)(2,1)} %query_ref.5, bf16[8192,128]{1,0:T(8,128)(2,1)} %key_ref.5, bf16[8192,128]{1,0:T(8,128)(2,1)} %value_ref.5), custom_call_target="tpu_custom_call" | custom-call | tf_op jit(solution)/shard_map/pallas_call | solution.py:146
  89.1 12.0 %collective-permute-done.4.right_ref = bf16[2,1024,256]{2,1,0:T(8,128)(2,1)} collective-permute-done((bf16[2,1024,256]{2,1,0:T(8,128)(2,1)}, bf16[2,1024,256]{2,1,0:T(8,128)(2,1)}, u32[]{:S(2)}, u32[]{:S(2)}) %collective-permute-start.4) | collective-permute-done | bytes 1048608 | tf_op jit(solution)/shard_map/ppermute | solution.py:270
  101.1 3.4 %collective-permute-done.3.left_ref = bf16[2,1024,256]{2,1,0:T(8,128)(2,1)} collective-permute-done((bf16[2,1024,256]{2,1,0:T(8,128)(2,1)}, bf16[2,1024,256]{2,1,0:T(8,128)(2,1)}, u32[]{:S(2)}, u32[]{:S(2)}) %collective-permute-start.3) | collective-permute-done | bytes 1048608 | tf_op jit(solution)/shard_map/ppermute | solution.py:270
  110.3 5.4 %collective-permute-done.8.near_ref = s16[3,272,1024]{2,1,0:T(8,128)(2,1)} collective-permute-done((s16[3,272,1024]{2,1,0:T(8,128)(2,1)}, s16[3,272,1024]{2,1,0:T(8,128)(2,1)}, u32[]{:S(2)}, u32[]{:S(2)}) %collective-permute-start.8) | collective-permute-done | bytes 1671200 | tf_op jit(solution)/shard_map/ppermute | solution.py:270
  115.7 1.9 %copy-done = f32[3,256,1024]{2,1,0:T(8,128)S(1)} copy-done((f32[3,256,1024]{2,1,0:T(8,128)S(1)}, f32[3,256,1024]{2,1,0:T(8,128)}, u32[]{:S(2)}) %copy-start) | copy-done | bytes 3145752
  117.6 3.7 %shard_map.114 = s16[4,272,1024]{2,1,0:T(8,128)(2,1)S(1)} custom-call(s32[3]{0:T(128)S(1)} %pad_add_fusion.2.places_ref.plan_ref, f32[3,256,1024]{2,1,0:T(8,128)S(1)} %copy-done, s16[3,272,1024]{2,1,0:T(8,128)(2,1)} %collective-permute-done.8.near_ref), custom_call_target="tpu_custom_call" | custom-call | tf_op jit(solution)/shard_map/pallas_call | solution.py:170
  122.7 5.2 %all-to-all-start.2 = ((s16[4,272,1024]{2,1,0:T(8,128)(2,1)}), s16[4,272,1024]{2,1,0:T(8,128)(2,1)}, u32[]{:S(2)}, u32[]{:S(2)}) async-start(s16[4,272,1024]{2,1,0:T(8,128)(2,1)} %copy-done.1), calls=%async_computation.2 | async-start | bytes 4456448 | tf_op jit(solution)/shard_map/all_to_all | solution.py:326
  129.3 7.3 %shard_map.116 = (f32[512,768]{1,0:T(8,128)}, f32[512,768]{1,0:T(8,128)S(1)}) custom-call(s32[9]{0:T(128)S(1)} %stack.119.plan_ref, bf16[2,1024,256]{2,1,0:T(8,128)(2,1)S(1)} %copy-done.2, bf16[2,1024,256]{2,1,0:T(8,128)(2,1)} %collective-permute-done.4.right_ref, bf16[1,1024,256]{2,1,0:T(8,128)(2,1)} %collective-permute-done.5.far_0_ref, ...), custom_call_target="tpu_custom_call" | custom-call | tf_op jit(solution)/shard_map/pallas_call | solution.py:234
  137.8 3.3 %shard_map.115 = f32[1,256,1024]{2,1,0:T(8,128)} custom-call(s32[1]{0:T(128)} %bitcast.order_ref, bf16[256,768]{1,0:T(8,128)(2,1)} %copy-done.5, bf16[8192,512]{1,0:T(8,128)(2,1)} %query_ref.5, bf16[8192,128]{1,0:T(8,128)(2,1)} %key_ref.5, bf16[8192,128]{1,0:T(8,128)(2,1)} %value_ref.5, s16[1,272,1024]{2,1,0:T(8,128)(2,1)} %collective-permute-done.7.refs_0_), custom_call_target="tpu_custom_call" | custom-call | tf_op jit(solution)/shard_map/pallas_call | solution.py:146
  142.6 3.8 %shard_map.117 = (f32[512,512]{1,0:T(8,128)}, f32[512,128]{1,0:T(8,128)}, f32[512,128]{1,0:T(8,128)}) custom-call(f32[512,768]{1,0:T(8,128)} %copy-done.3, f32[512,768]{1,0:T(8,128)} %copy-done.6), custom_call_target="tpu_custom_call" | custom-call | tf_op jit(solution)/shard_map/pallas_call | solution.py:259
  146.5 7.3 %all-to-all-done.2.refs_0_.refs_1_.refs_2_.refs_3_.refs_4_.refs_5_ = s16[4,272,1024]{2,1,0:T(8,128)(2,1)} async-done(((s16[4,272,1024]{2,1,0:T(8,128)(2,1)}), s16[4,272,1024]{2,1,0:T(8,128)(2,1)}, u32[]{:S(2)}, u32[]{:S(2)}) %all-to-all-start.2) | async-done | bytes 2228256 | tf_op jit(solution)/shard_map/all_to_all | solution.py:326
  153.7 3.9 %shard_map.118 = f32[256,1024]{1,0:T(8,128)} custom-call(s32[3]{0:T(128)} %copy-done.4, f32[256,1024]{1,0:T(8,128)} %bitcast.33, s16[4,272,1024]{2,1,0:T(8,128)(2,1)} %all-to-all-done.2.refs_0_.refs_1_.refs_2_.refs_3_.refs_4_.refs_5_, s16[4,272,1024]{2,1,0:T(8,128)(2,1)} %all-to-all-done.2.refs_0_.refs_1_.refs_2_.refs_3_.refs_4_.refs_5_, ...), custom_call_target="tpu_custom_call" | custom-call | tf_op jit(solution)/shard_map/pallas_call | solution.py:206
  (38 shorter events, 20.5 us)
Async XLA Ops:
  5.0 30.9 %all-to-all-start = ((bf16[16,32,1792]{2,1,0:T(8,128)(2,1)}), bf16[16,32,1792]{2,1,0:T(8,128)(2,1)S(1)}, u32[]{:S(2)}, u32[]{:S(2)}) async-start(bf16[16,32,1792]{2,1,0:T(8,128)(2,1)} %bitcast.31), calls=%async_computation | async-start | bytes 3670016 | tf_op jit(solution)/shard_map/all_to_all | solution.py:299
  36.3 12.2 %copy-start.5 = (bf16[256,768]{1,0:T(8,128)(2,1)}, bf16[256,768]{1,0:T(8,128)(2,1)S(1)}, u32[]{:S(2)}) copy-start(bf16[256,768]{1,0:T(8,128)(2,1)S(1)} %convolution_convert_fusion.1.rows_ref) | copy-start | bytes 1179652
  36.3 12.1 %collective-permute-start.2 = (bf16[256,768]{1,0:T(8,128)(2,1)S(1)}, bf16[256,768]{1,0:T(8,128)(2,1)S(1)}, u32[]{:S(2)}, u32[]{:S(2)}) collective-permute-start(bf16[256,768]{1,0:T(8,128)(2,1)S(1)} %convolution_convert_fusion.1.rows_ref), channel_id=1, source_target_pairs={{0,64},{64,0},{1,65},{65,1},{2,66},{66,2},{3,67},{67,3},{4,68},{68... | collective-permute-start | bytes 1179656 | tf_op jit(solution)/shard_map/ppermute | solution.py:270
  38.6 23.0 %collective-permute-start.1 = (bf16[1024,256]{1,0:T(8,128)(2,1)S(1)}, bf16[1024,256]{1,0:T(8,128)(2,1)S(1)}, u32[]{:S(2)}, u32[]{:S(2)}) collective-permute-start(bf16[1024,256]{1,0:T(8,128)(2,1)S(1)} %convolution_convert_fusion), channel_id=1, source_target_pairs={{0,1},{1,16},{2,35},{3,50},{4,68},{5,85},{6,102},{7,119},{8,9},{9,... | collective-permute-start | bytes 1572872 | tf_op jit(solution)/shard_map/ppermute | solution.py:280
  39.3 30.3 %collective-permute-start = (bf16[1024,256]{1,0:T(8,128)(2,1)S(1)}, bf16[1024,256]{1,0:T(8,128)(2,1)S(1)}, u32[]{:S(2)}, u32[]{:S(2)}) collective-permute-start(bf16[1024,256]{1,0:T(8,128)(2,1)S(1)} %convolution_convert_fusion), channel_id=1, source_target_pairs={{0,0},{1,17},{2,34},{3,51},{4,69},{5,84},{6,103},{7,118},{8,8},{9,... | collective-permute-start | bytes 1572872 | tf_op jit(solution)/shard_map/ppermute | solution.py:280
  70.6 52.2 %all-to-all-start.1 = ((bf16[4,2,256,768]{3,2,1,0:T(8,128)(2,1)}), bf16[4,2,256,768]{3,2,1,0:T(8,128)(2,1)S(1)}, u32[]{:S(2)}, u32[]{:S(2)}) async-start(bf16[4,2,256,768]{3,2,1,0:T(8,128)(2,1)} %broadcast_in_dim.2), calls=%async_computation.1 | async-start | bytes 6291456 | tf_op jit(solution)/shard_map/all_to_all | solution.py:315
  74.5 41.3 %collective-permute-start.8 = (s16[3,272,1024]{2,1,0:T(8,128)(2,1)}, s16[3,272,1024]{2,1,0:T(8,128)(2,1)}, u32[]{:S(2)}, u32[]{:S(2)}) collective-permute-start(s16[3,272,1024]{2,1,0:T(8,128)(2,1)} %get-tuple-element.36), channel_id=1, source_target_pairs={{0,1},{1,0},{2,3},{3,2},{4,5},{5,4},{6,7},{7,6},{8,9},{9,8},{10,11... | collective-permute-start | bytes 5013512 | tf_op jit(solution)/shard_map/ppermute | solution.py:270
  76.6 24.5 %collective-permute-start.4 = (bf16[2,1024,256]{2,1,0:T(8,128)(2,1)}, bf16[2,1024,256]{2,1,0:T(8,128)(2,1)}, u32[]{:S(2)}, u32[]{:S(2)}) collective-permute-start(bf16[2,1024,256]{2,1,0:T(8,128)(2,1)} %pad_maximum_fusion.pair_ref), channel_id=1, source_target_pairs={{0,6},{2,0},{4,2},{6,4},{1,7},{3,1},{5,3},{7,5},{8,14},{10,8},{12,... | collective-permute-start | bytes 3145736 | tf_op jit(solution)/shard_map/ppermute | solution.py:270
  78.5 26.0 %collective-permute-start.3 = (bf16[2,1024,256]{2,1,0:T(8,128)(2,1)}, bf16[2,1024,256]{2,1,0:T(8,128)(2,1)}, u32[]{:S(2)}, u32[]{:S(2)}) collective-permute-start(bf16[2,1024,256]{2,1,0:T(8,128)(2,1)} %pad_maximum_fusion.pair_ref), channel_id=1, source_target_pairs={{0,2},{2,4},{4,6},{6,0},{1,3},{3,5},{5,7},{7,1},{8,10},{10,12},{12... | collective-permute-start | bytes 3145736 | tf_op jit(solution)/shard_map/ppermute | solution.py:270
  78.6 49.4 %collective-permute-start.7 = (s16[1,272,1024]{2,1,0:T(8,128)(2,1)}, s16[1,272,1024]{2,1,0:T(8,128)(2,1)}, u32[]{:S(2)}, u32[]{:S(2)}) collective-permute-start(s16[1,272,1024]{2,1,0:T(8,128)(2,1)} %get-tuple-element.34), channel_id=1, source_target_pairs={{0,1},{1,0},{2,3},{3,2},{4,5},{5,4},{6,7},{7,6},{8,9},{9,8},{10,11... | collective-permute-start | bytes 1671176 | tf_op jit(solution)/shard_map/ppermute | solution.py:270
  108.2 19.8 %collective-permute-start.6 = (bf16[1,1024,256]{2,1,0:T(8,128)(2,1)}, bf16[1,1024,256]{2,1,0:T(8,128)(2,1)}, u32[]{:S(2)}, u32[]{:S(2)}) collective-permute-start(bf16[1,1024,256]{2,1,0:T(8,128)(2,1)} %slice.19), channel_id=1, source_target_pairs={{0,6},{2,0},{4,2},{6,4},{1,7},{3,1},{5,3},{7,5},{8,14},{10,8},{12,... | collective-permute-start | bytes 1572872 | tf_op jit(solution)/shard_map/ppermute | solution.py:270
  108.5 19.5 %collective-permute-start.5 = (bf16[1,1024,256]{2,1,0:T(8,128)(2,1)}, bf16[1,1024,256]{2,1,0:T(8,128)(2,1)}, u32[]{:S(2)}, u32[]{:S(2)}) collective-permute-start(bf16[1,1024,256]{2,1,0:T(8,128)(2,1)} %slice.18), channel_id=1, source_target_pairs={{0,2},{2,4},{4,6},{6,0},{1,3},{3,5},{5,7},{7,1},{8,10},{10,12},{12... | collective-permute-start | bytes 1572872 | tf_op jit(solution)/shard_map/ppermute | solution.py:270
  110.3 11.0 %copy-start.4 = (s32[3]{0:T(128)}, s32[3]{0:T(128)S(1)}, u32[]{:S(2)}) copy-start(s32[3]{0:T(128)S(1)} %pad_add_fusion.2.places_ref.plan_ref) | copy-start | bytes 40
  115.7 1.9 %copy-start = (f32[3,256,1024]{2,1,0:T(8,128)S(1)}, f32[3,256,1024]{2,1,0:T(8,128)}, u32[]{:S(2)}) copy-start(f32[3,256,1024]{2,1,0:T(8,128)} %shard_map.113.own_ref) | copy-start | bytes 9437188
  121.3 1.4 copy-start.1
  122.7 31.0 %all-to-all-start.2 = ((s16[4,272,1024]{2,1,0:T(8,128)(2,1)}), s16[4,272,1024]{2,1,0:T(8,128)(2,1)}, u32[]{:S(2)}, u32[]{:S(2)}) async-start(s16[4,272,1024]{2,1,0:T(8,128)(2,1)} %copy-done.1), calls=%async_computation.2 | async-start | bytes 4456448 | tf_op jit(solution)/shard_map/all_to_all | solution.py:326
  128.0 1.2 copy-start.2
  136.6 1.2 copy-start.3
  137.8 3.6 %collective-permute-start.9 = (f32[512,768]{1,0:T(8,128)}, f32[512,768]{1,0:T(8,128)S(1)}, u32[]{:S(2)}, u32[]{:S(2)}) collective-permute-start(f32[512,768]{1,0:T(8,128)} %get-tuple-element.42), channel_id=1, source_target_pairs={{0,8},{8,0},{1,9},{9,1},{2,10},{10,2},{3,11},{11,3},{4,12},{12,4},... | collective-permute-start | bytes 4718600 | tf_op jit(solution)/shard_map/ppermute | solution.py:270
  141.4 1.2 copy-start.6
